TPU v7x, 128 devices: a whole 4x4x4 slice. The times are simulated.
128 devices in a mesh: boxes: 128 (over x, z, y, core).
Axes of the slice: x: 4, y: 4, z: 4, core: 2. Of those that a mesh axis runs over, the one named last changes fastest.
Arguments:
- old_state: float32 [2048, 5, 4096], P('boxes'), may hold values from -6 to 6
- old_map: int32 [2048], replicated, may hold values from 0 to 2047, as said below
- new_map: int32 [2048], replicated, may hold values from 0 to 2047, as said below
- box_level: int32 [2048], replicated, may hold values from 0 to 1, as said below
- ghost_list: int32 [2048, 6, 4], replicated, may hold values from -1 to 2047, as said below
- coupling: float32 [3, 5, 5], replicated, may hold values from -2.5 to 2.5
Outputs:
- stepped: float32 [2048, 5, 4096], P('boxes')
Inputs may be any that keep to these rules, and one draw needn't show every extreme that they name: A permutation: old slot s holds box old_map[s]. Each device sends exactly 1 of its boxes to each of 16 devices (itself possibly among them) and none to the others. A permutation: new slot t holds box new_map[t]. `box_level`: 1 for the fine boxes of the wall slab, half of all boxes; 0 for the coarse boxes. ghost_list[b, f] = (g, p, o1, o2): g is the source box or -1 at a wall, p lies in 0 to 15; where box_level[g] equals box_level[b], o1 = o2 = 0; otherwise box_level[g] = box_level[b] - 1 and o1, o2 are 0 or 8. The source of every ghost plane is owned under new_map by the target box's owner or by a device at most two indices away along the axis, counting around the end; at most 20 planes of one device are needed by another, a number reached in every draw.
All inputs are finite; a program needn't handle non-finite values.
Results may differ from a plain program's by a relative error of at most 0.0003.
Values sent between devices are 32-bit elements; how exact they have to be, the bound alone decides.
A program may use at most 256 MiB of HBM per device.

v0:
```python
import jax
import jax.numpy as jnp
from jax import lax
from jax.sharding import PartitionSpec as P

E = 16
GCAP = 20


diffusion_number = 0.12
advection_number = 0.25


def shifted(value, axis, steps):
    count = lax.axis_size(axis)
    pairs = [(source, (source + steps) % count) for source in range(count)]
    return lax.ppermute(value, axis, pairs)


def mix_fields(matrix, field):
    return jnp.einsum("gf,fxyz->gxyz", matrix, field, precision=lax.Precision.HIGHEST)


def increment_from(padded, cells, scale, coupling):
    lower_first = padded[:, :-2, 1:-1, 1:-1]
    upper_first = padded[:, 2:, 1:-1, 1:-1]
    lower_second = padded[:, 1:-1, :-2, 1:-1]
    upper_second = padded[:, 1:-1, 2:, 1:-1]
    lower_third = padded[:, 1:-1, 1:-1, :-2]
    upper_third = padded[:, 1:-1, 1:-1, 2:]
    laplace = (
        upper_first
        + lower_first
        + (upper_second + lower_second)
        + (upper_third + lower_third)
        - 6.0 * cells
    )
    flux = mix_fields(coupling[0], upper_first - lower_first)
    flux = flux + mix_fields(coupling[1], upper_second - lower_second)
    flux = flux + mix_fields(coupling[2], upper_third - lower_third)
    return diffusion_number / (scale * scale) * laplace - advection_number / scale * 0.5 * flux


def surround(cells, ghosts):
    fields, edge = (cells.shape[0], cells.shape[1])
    inner = jnp.concatenate([ghosts[4][:, :, :, None], cells, ghosts[5][:, :, :, None]], 3)
    zero_third = jnp.zeros((fields, edge, 1), jnp.float32)
    lower_second = jnp.concatenate([zero_third, ghosts[2], zero_third], 2)[:, :, None, :]
    upper_second = jnp.concatenate([zero_third, ghosts[3], zero_third], 2)[:, :, None, :]
    inner = jnp.concatenate([lower_second, inner, upper_second], 2)
    lower_first = jnp.pad(ghosts[0], ((0, 0), (1, 1), (1, 1)))[:, None]
    upper_first = jnp.pad(ghosts[1], ((0, 0), (1, 1), (1, 1)))[:, None]
    return jnp.concatenate([lower_first, inner, upper_first], 1)


def stencil_step(cells, ghosts, scale, coupling):
    padded = surround(cells, ghosts)
    return cells + increment_from(padded, cells, scale, coupling)


def requests_of(receiver, new_map, new_place, box_level, ghost_list, per_device):
    boxes = lax.dynamic_slice_in_dim(new_map, receiver * per_device, per_device)
    entries = ghost_list[boxes]
    source = entries[:, :, 0]
    valid = source >= 0
    source_id = jnp.maximum(source, 0)
    holder_slot = new_place[source_id]
    ratio = jnp.where(box_level[source_id] < box_level[boxes][:, None], 2, 1).astype(jnp.int32)
    axis_id = jnp.broadcast_to(jnp.arange(6, dtype=jnp.int32) // 2, source.shape)
    return (
        valid.reshape(-1),
        (holder_slot // per_device).reshape(-1),
        (holder_slot % per_device).reshape(-1),
        axis_id.reshape(-1),
        entries[:, :, 1].reshape(-1),
        entries[:, :, 2].reshape(-1),
        entries[:, :, 3].reshape(-1),
        ratio.reshape(-1),
    )


def planes_for(flat_cells, wanted, picks, edge):
    volume = edge * edge * edge
    slot = wanted[2][picks]
    axis_id = wanted[3][picks][:, None, None]
    plane_index = wanted[4][picks][:, None, None]
    ratio = wanted[7][picks][:, None]
    counter = jnp.arange(edge, dtype=jnp.int32)[None, :]
    first = wanted[5][picks][:, None] + counter // ratio
    second = wanted[6][picks][:, None] + counter // ratio
    along_u = first[:, :, None]
    along_v = second[:, None, :]
    index_first = (plane_index * edge + along_u) * edge + along_v
    index_second = (along_u * edge + plane_index) * edge + along_v
    index_third = (along_u * edge + along_v) * edge + plane_index
    cell_index = jnp.where(
        axis_id == 0, index_first, jnp.where(axis_id == 1, index_second, index_third)
    )
    where_flat = slot[:, None, None] * volume + cell_index
    count = picks.shape[0]
    fields = flat_cells.shape[0]
    taken = flat_cells[:, where_flat.reshape(-1)]
    return taken.reshape(fields, count, edge, edge).transpose(1, 0, 2, 3)


def send_planes(planes, distance):
    return shifted(planes, "boxes", distance)


def shards(old_state, old_map, new_map, box_level, ghost_list, coupling):
    devices = lax.axis_size("boxes")
    device_index = lax.axis_index("boxes")
    per_device, fields, volume = old_state.shape
    edge = E
    total = old_map.shape[0]
    capacity = max(1, 2 * per_device // devices)
    plane_room = GCAP
    requests = 6 * per_device
    slots = jnp.arange(total, dtype=jnp.int32)
    old_place = jnp.zeros((total,), jnp.int32).at[old_map].set(slots)
    new_place = jnp.zeros((total,), jnp.int32).at[new_map].set(slots)
    target_device = (new_place[old_map] // per_device).reshape(devices, per_device)
    counter = jnp.arange(per_device, dtype=jnp.int32)
    earlier = counter[None, :] < counter[:, None]
    send_rank = jnp.sum(
        ((target_device[:, :, None] == target_device[:, None, :]) & earlier[None]).astype(
            jnp.int32
        ),
        axis=2,
    )
    own_targets = lax.dynamic_index_in_dim(target_device, device_index, 0, False)
    own_ranks = lax.dynamic_index_in_dim(send_rank, device_index, 0, False)
    table = (
        jnp.full((devices * capacity,), per_device, jnp.int32)
        .at[own_targets * capacity + own_ranks]
        .set(counter)
    )
    filled = table < per_device
    picked = jnp.minimum(table, per_device - 1)
    outgoing = jnp.where(filled[:, None, None], old_state[picked], 0.0).reshape(
        devices, capacity, fields, volume
    )
    own_boxes = lax.dynamic_slice_in_dim(new_map, device_index * per_device, per_device)
    anchor = old_place[own_boxes]
    position = anchor // per_device * capacity + send_rank.reshape(total)[anchor]
    own_scale = (2 - box_level[own_boxes]).astype(jnp.float32)
    arrived = lax.all_to_all(outgoing, "boxes", split_axis=0, concat_axis=0, tiled=True)
    regridded = arrived.reshape(-1, fields, volume)[position]
    cells = regridded.reshape(per_device, fields, edge, edge, edge)
    flat_cells = regridded.transpose(1, 0, 2).reshape(fields, per_device * volume)
    mine = requests_of(device_index, new_map, new_place, box_level, ghost_list, per_device)
    every_request = jnp.arange(requests, dtype=jnp.int32)
    local_planes = planes_for(flat_cells, mine, every_request, edge)
    local_used = mine[0] & (mine[1] == device_index)
    ghosts = jnp.where(local_used[:, None, None, None], local_planes, 0.0)
    for distance in (1, 2, -1, -2):
        receiver = (device_index + distance) % devices
        wanted = requests_of(receiver, new_map, new_place, box_level, ghost_list, per_device)
        chosen = wanted[0] & (wanted[1] == device_index)
        order_index = jnp.cumsum(chosen.astype(jnp.int32)) - 1
        slot_table = (
            jnp.full((plane_room,), requests, jnp.int32)
            .at[jnp.where(chosen, order_index, plane_room)]
            .set(every_request, mode="drop")
        )
        used = slot_table < requests
        planes = planes_for(flat_cells, wanted, jnp.minimum(slot_table, requests - 1), edge)
        planes = jnp.where(used[:, None, None, None], planes, 0.0).reshape(
            plane_room, fields, edge * edge
        )
        incoming = send_planes(planes, distance).reshape(plane_room, fields, edge, edge)
        sender = (device_index - distance) % devices
        taken = mine[0] & (mine[1] == sender)
        arrival_rank = jnp.clip(jnp.cumsum(taken.astype(jnp.int32)) - 1, 0, plane_room - 1)
        ghosts = ghosts + jnp.where(taken[:, None, None, None], incoming[arrival_rank], 0.0)
    ghosts = ghosts.reshape(per_device, 6, fields, edge, edge)
    stepped = jax.vmap(stencil_step, in_axes=(0, 0, 0, None))(cells, ghosts, own_scale, coupling)
    stepped = stepped.reshape(per_device, fields, volume)
    return stepped


def solution(mesh):
    return jax.shard_map(
        shards,
        mesh=mesh,
        in_specs=(P("boxes", None, None), P(), P(), P(), P(), P()),
        out_specs=P("boxes", None, None),
        check_vma=False,
    )
```

profile of v0, /device:TPU:0, one launch (start us, length us, event | category | flops | bytes accessed | tf_op | source)
XLA Modules:
  0.0 883.3 jit_solution(11663977535513729925)
XLA Ops:
  2.4 8.0 scatter_custom_fusion
  10.5 11.8 %gather_fusion = s32[2048]{0:T(1024)S(1)} fusion(s32[2048]{0:T(1024)S(1)} %scatter_custom_fusion, s32[2048]{0:T(1024)S(1)} %get-tuple-element.58), kind=kCustom, calls=%fused_computation | custom fusion | bytes 24576 | tf_op jit(solution)/shard_map/gather | solution.py:122
  22.4 8.0 scatter_custom_fusion.2
  32.6 19.2 %gather_fusion.1 = f32[128,5,4096]{2,0,1:T(8,128)} fusion(f32[16,5,4096]{2,0,1:T(8,128)S(1)} %copy-done, s32[1024]{0:T(1024)S(1)} %pad_clamp_fusion.21), kind=kCustom, calls=%fused_computation.1 | custom fusion | bytes 20972032 | tf_op jit(solution)/shard_map/gather | solution.py:140
  51.8 5.0 bitcast_select_fusion
  56.9 13.2 %copy.669 = f32[128,1,5,4096]{3,1,2,0:T(1,128)} copy(f32[128,1,5,4096]{3,0,2,1:T(8,128)S(1)} %bitcast_select_fusion) | data formatting | bytes 20971520 | tf_op jit(solution)/shard_map/jit(_where)/select_n | solution.py:140
  70.0 11.7 %all-to-all-start = ((f32[128,1,5,4096]{3,1,2,0:T(1,128)}), f32[128,1,5,4096]{3,1,2,0:T(1,128)}, u32[]{:S(2)}, u32[]{:S(2)}) async-start(f32[128,1,5,4096]{3,1,2,0:T(1,128)} %copy.669), calls=%async_computation | async-start | bytes 20971520 | tf_op jit(solution)/shard_map/all_to_all | solution.py:147
  160.3 56.4 %all-to-all-done = f32[128,1,5,4096]{3,1,2,0:T(1,128)} async-done(((f32[128,1,5,4096]{3,1,2,0:T(1,128)}), f32[128,1,5,4096]{3,1,2,0:T(1,128)}, u32[]{:S(2)}, u32[]{:S(2)}) %all-to-all-start) | async-done | bytes 10485792 | tf_op jit(solution)/shard_map/all_to_all | solution.py:147
  216.6 20.2 %copy.767 = f32[128,1,5,4096]{3,2,0,1:T(8,128)} copy(f32[128,1,5,4096]{3,1,2,0:T(1,128)} %all-to-all-done) | data formatting | bytes 20971520 | tf_op jit(solution)/shard_map/reshape | solution.py:148
  236.8 6.4 gather_fusion.4
  243.3 16.9 %copy.679 = f32[5,65536]{0,1:T(8,128)} copy(f32[5,65536]{1,0:T(8,128)S(1)} %bitcast.197) | data formatting | bytes 2621440 | tf_op jit(solution)/shard_map/reshape | solution.py:150
  260.2 28.2 %gather_fusion.62 = f32[5120,5]{1,0:T(8,128)} fusion(f32[5,65536]{0,1:T(8,128)} %copy.679, s32[5120]{0:T(1024)S(1)} %broadcast_clamp_fusion.1), kind=kCustom, calls=%fused_computation.62 | custom fusion | bytes 225280 | tf_op jit(solution)/shard_map/gather | solution.py:102
  288.3 4.5 copy.722
  294.5 28.2 %gather_fusion.50 = f32[5120,5]{1,0:T(8,128)} fusion(f32[5,65536]{0,1:T(8,128)} %copy.679, s32[5120]{0:T(1024)S(1)} %broadcast_clamp_fusion.2), kind=kCustom, calls=%fused_computation.50 | custom fusion | bytes 225280 | tf_op jit(solution)/shard_map/gather | solution.py:102
  322.7 4.5 copy.712
  331.6 28.2 %gather_fusion.38 = f32[5120,5]{1,0:T(8,128)} fusion(f32[5,65536]{0,1:T(8,128)} %copy.679, s32[5120]{0:T(1024)S(1)} %broadcast_clamp_fusion.3), kind=kCustom, calls=%fused_computation.38 | custom fusion | bytes 225280 | tf_op jit(solution)/shard_map/gather | solution.py:102
  359.7 4.5 copy.702
  366.5 28.4 %gather_fusion.26 = f32[5120,5]{1,0:T(8,128)} fusion(f32[5,65536]{0,1:T(8,128)} %copy.679, s32[5120]{0:T(1024)S(1)} %broadcast_clamp_fusion.4), kind=kCustom, calls=%fused_computation.26 | custom fusion | bytes 225280 | tf_op jit(solution)/shard_map/gather | solution.py:102
  394.8 4.5 copy.688
  402.2 5.7 reshape.2621
  407.9 16.8 %copy.740 = f32[16,5,16,16,16]{4,1,3,2,0:T(8,128)} copy(f32[16,5,16,16,16]{4,3,2,1,0:T(8,128)} %reshape.2621) | data formatting | bytes 2621440 | tf_op jit(solution)/shard_map/reshape | solution.py:149
  424.7 91.8 %gather_fusion.15 = f32[24576,5]{1,0:T(8,128)} fusion(f32[5,65536]{0,1:T(8,128)} %copy.679, s32[24576]{0:T(1024)S(1)} %broadcast_clamp_fusion), kind=kCustom, calls=%fused_computation.15 | custom fusion | bytes 1081344 | tf_op jit(solution)/shard_map/gather | solution.py:102
  516.5 13.1 %copy.680 = f32[5,96,16,16]{3,2,0,1:T(8,128)} copy(f32[5,96,16,16]{0,3,2,1:T(8,128)} %bitcast.199) | data formatting | bytes 983040 | tf_op jit(solution)/shard_map/reshape | solution.py:103
  537.9 4.0 gather_fusion.27
  550.3 8.0 fusion.11
  563.3 11.3 %copy.728 = f32[16,5,16,16,1]{4,1,3,2,0:T(8,128)} copy(f32[16,5,16,16,1]{3,2,1,0,4:T(8,128)} %get-tuple-element.41) | data formatting | bytes 163840 | tf_op jit(solution)/shard_map/vmap()/broadcast_in_dim;vmap()/squeeze | solution.py:46
  574.6 10.4 %copy.726 = f32[16,5,16,16,1]{4,1,3,2,0:T(8,128)} copy(f32[16,5,16,16,1]{3,2,1,0,4:T(8,128)S(1)} %copy-done.3) | data formatting | bytes 163840 | tf_op jit(solution)/shard_map/vmap()/broadcast_in_dim;vmap()/squeeze | solution.py:46
  587.4 36.4 %fusion.1 = f32[16,16,16,16,5]{3,4,2,1,0:T(8,128)} fusion(f32[16,5,16,16,1]{4,1,3,2,0:T(8,128)} %copy.728, f32[16,5,16,16,16]{4,1,3,2,0:T(8,128)} %copy.740, f32[16,5,16,16,1]{4,1,3,2,0:T(8,128)} %copy.726, f32[1,5,5]{2,0,1:T(1,128)S(1)} %get-tuple-element.51), kind=kOutput, calls=%fused_computation.92 | convolution fusion | flops 20643840 | bytes 2785380 | tf_op jit(solution)/shard_map/vmap(gf,fxyz->gxyz)/dot_general | solution.py:21
  623.9 38.3 %fusion.3 = f32[16,16,16,16,5]{3,4,2,1,0:T(8,128)} fusion(f32[1,5,5]{2,0,1:T(1,128)S(1)} %copy-done.10, f32[16,5,16,1,18]{4,1,3,2,0:T(8,128)S(1)} %copy-done.6, f32[16,5,16,16,1]{4,1,3,2,0:T(8,128)} %copy.728, f32[16,5,16,16,16]{4,1,3,2,0:T(8,128)} %copy.740, f32[16,5,16,16,1]{4,1,3,2,0:T(8,128)} %copy.726, f32[16,5,16,1,18]{4,1,3,2,0:T(8,128)S(1)} %copy-done.5), kind=kOutput, calls=%fused_computation.94 | convolution fusion | flops 21954560 | bytes 2969700 | tf_op jit(solution)/shard_map/vmap(gf,fxyz->gxyz)/dot_general | solution.py:21
  662.3 198.6 %fusion = f32[16,5,16,16,16]{4,1,3,2,0:T(8,128)} fusion(f32[16,5,16,16,16]{4,1,3,2,0:T(8,128)} %copy.740, f32[16,16,16,16,5]{3,4,2,1,0:T(8,128)} %fusion.1, f32[16,16,16,16,5]{3,4,2,1,0:T(8,128)} %fusion.3, f32[16,5,1,18,18]{4,1,3,2,0:T(8,128)} %pad_bitcast_fusion.1, f32[16,5,16,1,18]{4,1,3,2,0:T(8,128)} %get-tuple-element.44, ...), kind=kOutput, calls=%fused_computation.90 | convolution fusion | flops 33423360 | bytes 5798628 | tf_op jit(solution)/shard_map/vmap(gf,fxyz->gxyz)/dot_general | solution.py:21
  861.0 11.8 %copy.741 = f32[16,5,16,16,16]{4,3,2,0,1:T(8,128)} copy(f32[16,5,16,16,16]{4,1,3,2,0:T(8,128)} %fusion) | data formatting | bytes 2621440 | tf_op jit(solution)/shard_map/vmap()/add | solution.py:58
  872.7 10.3 %reshape.1980 = f32[16,5,4096]{2,0,1:T(8,128)} reshape(f32[16,5,16,16,16]{4,3,2,0,1:T(8,128)} %copy.741) | data formatting | bytes 2621440 | tf_op jit(solution)/shard_map/reshape | solution.py:178
  (318 shorter events, 117.5 us)
Async XLA Ops:
  0.0 32.6 %copy-start = (f32[16,5,4096]{2,0,1:T(8,128)S(1)}, f32[16,5,4096]{2,0,1:T(8,128)}, u32[]{:S(2)}) copy-start(f32[16,5,4096]{2,0,1:T(8,128)} %param.10) | copy-start | bytes 3932164
  56.9 25.0 %copy-start.2 = (s32[2048]{0:T(1024)S(1)}, s32[2048]{0:T(1024)}, u32[]{:S(2)}) copy-start(s32[2048]{0:T(1024)} %param.13) | copy-start | bytes 24580
  56.9 27.0 %copy-start.7 = (s32[2048,6,4]{0,2,1:T(4,128)S(1)}, s32[2048,6,4]{0,2,1:T(4,128)}, u32[]{:S(2)}) copy-start(s32[2048,6,4]{0,2,1:T(4,128)} %param.14) | copy-start | bytes 589828
  70.0 146.6 %all-to-all-start = ((f32[128,1,5,4096]{3,1,2,0:T(1,128)}), f32[128,1,5,4096]{3,1,2,0:T(1,128)}, u32[]{:S(2)}, u32[]{:S(2)}) async-start(f32[128,1,5,4096]{3,1,2,0:T(1,128)} %copy.669), calls=%async_computation | async-start | bytes 20971520 | tf_op jit(solution)/shard_map/all_to_all | solution.py:147
  110.2 13.7 %copy-start.8 = (f32[3,5,5]{2,0,1:T(4,128)S(1)}, f32[3,5,5]{2,0,1:T(4,128)}, u32[]{:S(2)}) copy-start(f32[3,5,5]{2,0,1:T(4,128)} %param.15) | copy-start | bytes 904
  294.4 235.2 %collective-permute-start.3 = (f32[20,5,256]{2,0,1:T(8,128)S(1)}, f32[20,5,256]{2,0,1:T(8,128)S(1)}, u32[]{:S(2)}, u32[]{:S(2)}) collective-permute-start(f32[20,5,256]{2,0,1:T(8,128)S(1)} %reshape.1977), channel_id=1, source_target_pairs={{0,126},{1,127},{2,0},{3,1},{4,2},{5,3},{6,4},{7,5},{8,6},{9,7},{1... | collective-permute-start | bytes 307208 | tf_op jit(solution)/shard_map/ppermute | solution.py:17
  328.8 201.2 %collective-permute-start.2 = (f32[20,5,256]{2,0,1:T(8,128)S(1)}, f32[20,5,256]{2,0,1:T(8,128)S(1)}, u32[]{:S(2)}, u32[]{:S(2)}) collective-permute-start(f32[20,5,256]{2,0,1:T(8,128)S(1)} %reshape.1974), channel_id=1, source_target_pairs={{0,127},{1,0},{2,1},{3,2},{4,3},{5,4},{6,5},{7,6},{8,7},{9,8},{10,... | collective-permute-start | bytes 307208 | tf_op jit(solution)/shard_map/ppermute | solution.py:17
  366.5 163.9 %collective-permute-start.1 = (f32[20,5,256]{2,0,1:T(8,128)}, f32[20,5,256]{2,0,1:T(8,128)}, u32[]{:S(2)}, u32[]{:S(2)}) collective-permute-start(f32[20,5,256]{2,0,1:T(8,128)} %reshape.1971), channel_id=1, source_target_pairs={{0,2},{1,3},{2,4},{3,5},{4,6},{5,7},{6,8},{7,9},{8,10},{9,11},{10,... | collective-permute-start | bytes 307208 | tf_op jit(solution)/shard_map/ppermute | solution.py:17
  401.6 132.0 %collective-permute-start = (f32[20,5,256]{2,0,1:T(8,128)}, f32[20,5,256]{2,0,1:T(8,128)}, u32[]{:S(2)}, u32[]{:S(2)}) collective-permute-start(f32[20,5,256]{2,0,1:T(8,128)} %reshape.1968), channel_id=1, source_target_pairs={{0,1},{1,2},{2,3},{3,4},{4,5},{5,6},{6,7},{7,8},{8,9},{9,10},{10,1... | collective-permute-start | bytes 307208 | tf_op jit(solution)/shard_map/ppermute | solution.py:17
  535.7 14.5 %copy-start.11 = (pred[96]{0:T(512)(128)(4,1)S(1)}, pred[96]{0:T(512)(128)(4,1)}, u32[]{:S(2)}) copy-start(pred[96]{0:T(512)(128)(4,1)} %get-tuple-element.27) | copy-start | bytes 292
  535.7 14.5 %copy-start.12 = (pred[96]{0:T(512)(128)(4,1)S(1)}, pred[96]{0:T(512)(128)(4,1)}, u32[]{:S(2)}) copy-start(pred[96]{0:T(512)(128)(4,1)} %get-tuple-element.79) | copy-start | bytes 292
  535.7 14.5 %copy-start.13 = (pred[96]{0:T(512)(128)(4,1)S(1)}, pred[96]{0:T(512)(128)(4,1)}, u32[]{:S(2)}) copy-start(pred[96]{0:T(512)(128)(4,1)} %get-tuple-element.80) | copy-start | bytes 292
  535.7 14.5 %copy-start.14 = (pred[96]{0:T(512)(128)(4,1)S(1)}, pred[96]{0:T(512)(128)(4,1)}, u32[]{:S(2)}) copy-start(pred[96]{0:T(512)(128)(4,1)} %get-tuple-element.81) | copy-start | bytes 292
  535.7 14.5 %copy-start.15 = (pred[96]{0:T(512)(128)(4,1)S(1)}, pred[96]{0:T(512)(128)(4,1)}, u32[]{:S(2)}) copy-start(pred[96]{0:T(512)(128)(4,1)} %get-tuple-element.82) | copy-start | bytes 292
  562.8 11.9 %copy-start.3 = (f32[16,5,16,16,1]{3,2,1,0,4:T(8,128)S(1)}, f32[16,5,16,16,1]{3,2,1,0,4:T(8,128)}, u32[]{:S(2)}) copy-start(f32[16,5,16,16,1]{3,2,1,0,4:T(8,128)} %get-tuple-element.42) | copy-start | bytes 245764
  587.4 36.4 %copy-start.5 = (f32[16,5,16,1,18]{4,1,3,2,0:T(8,128)S(1)}, f32[16,5,16,1,18]{4,1,3,2,0:T(8,128)}, u32[]{:S(2)}) copy-start(f32[16,5,16,1,18]{4,1,3,2,0:T(8,128)} %get-tuple-element.43) | copy-start | bytes 276484
  587.4 36.4 %copy-start.6 = (f32[16,5,16,1,18]{4,1,3,2,0:T(8,128)S(1)}, f32[16,5,16,1,18]{4,1,3,2,0:T(8,128)}, u32[]{:S(2)}) copy-start(f32[16,5,16,1,18]{4,1,3,2,0:T(8,128)} %get-tuple-element.44) | copy-start | bytes 276484
  587.4 36.5 %copy-start.10 = (f32[1,5,5]{2,0,1:T(1,128)S(1)}, f32[1,5,5]{2,0,1:T(1,128)}, u32[]{:S(2)}) copy-start(f32[1,5,5]{2,0,1:T(1,128)} %get-tuple-element.50) | copy-start | bytes 304
  623.9 38.4 %copy-start.4 = (f32[16,5,1,18,18]{4,1,3,2,0:T(8,128)S(1)}, f32[16,5,1,18,18]{4,1,3,2,0:T(8,128)}, u32[]{:S(2)}) copy-start(f32[16,5,1,18,18]{4,1,3,2,0:T(8,128)} %pad_bitcast_fusion) | copy-start | bytes 311044
  623.9 38.4 %copy-start.9 = (f32[1,5,5]{2,0,1:T(1,128)S(1)}, f32[1,5,5]{2,0,1:T(1,128)}, u32[]{:S(2)}) copy-start(f32[1,5,5]{2,0,1:T(1,128)} %get-tuple-element.49) | copy-start | bytes 304
  623.9 38.4 %copy-start.16 = (f32[16]{0:T(128)S(1)}, f32[16]{0:T(128)}, u32[]{:S(2)}) copy-start(f32[16]{0:T(128)} %get-tuple-element.83) | copy-start | bytes 196
  623.9 38.4 %copy-start.17 = (f32[16]{0:T(128)S(1)}, f32[16]{0:T(128)}, u32[]{:S(2)}) copy-start(f32[16]{0:T(128)} %get-tuple-element.84) | copy-start | bytes 196
  662.3 220.8 %copy-start.1 = (f32[16,5,4096]{2,0,1:T(8,128)S(1)}, f32[16,5,4096]{2,0,1:T(8,128)}, u32[]{:S(2)}) copy-start(f32[16,5,4096]{2,0,1:T(8,128)} %param.10) | copy-start | bytes 3932164
where the time goes:
time: 889 us; the launch traced here: 883 us
  local copies, waits for them, and re-layouts  502 us (56%)
  matrix products  273 us (31%)
  waiting for transfers between devices  56.4 us (6%)
  other arithmetic  35 us (4%)
  starting transfers between devices  14.6 us (2%)
    dot_general x3, matrix products, mix_fields(): jnp.einsum('gf,fxyz->gxyz', matrix, field, precision=lax.Precision.HIGHEST)  273 us
    gather x5, local copies, waits for them, and re-layouts, planes_for(): taken = flat_cells[:, where_flat.reshape(-1)]  205 us
    all_to_all x1, waiting for transfers between devices, shards(): lax.all_to_all(outgoing, 'boxes', split_axis=0, concat_axis=0, tiled=True)  56.4 us
    reshape x5, local copies, waits for them, and re-layouts, planes_for(): return taken.reshape(fields, count, edge, edge).transpose(1, 0, 2, 3)  31 us
    reshape x2, local copies, waits for them, and re-layouts, shards(): cells = regridded.reshape(per_device, fields, edge, edge, edge)  22.5 us
    reshape x1, local copies, waits for them, and re-layouts, shards(): regridded = arrived.reshape(-1, fields, volume)[position]  20.2 us
    gather x1, local copies, waits for them, and re-layouts, shards(): old_state[picked]  19.2 us
  transfers between devices with their start and end apart: 5, of which 1 were waited for; matrix products, arithmetic and copies ran while one was open for 36% of the time, Pallas kernels for 0%

commit v1 on v0

--- a/solution.py
+++ b/solution.py
@@ -1,7 +1,201 @@
+import functools
+
 import jax
 import jax.numpy as jnp
 from jax import lax
+from jax.experimental import pallas as pl
+from jax.experimental.pallas import tpu as pltpu
+
 from jax.sharding import PartitionSpec as P
+
+MESH = pl.DeviceIdType.MESH
+N = 128
+STRIDE = 37
+
+
+def partner(me, k):
+    return lax.rem(me + k * STRIDE, N)
+
+
+def bytes_of(ref, sem):
+    return pltpu.make_async_copy(ref, ref, sem)
+
+
+def kernel(state, old_map, new_map, out, tiles, send_a, send_ar, recv_a, recv_ar, rolled, send_b, send_br,
+           recv_br, cells, src_v, src_s, load_sem, send_sem, recv_sem, small_sem):
+    me = lax.axis_index("boxes")
+    barrier = pltpu.get_barrier_semaphore()
+
+    def greet(k, c):
+        pl.semaphore_signal(barrier, inc=1, device_id=(partner(me, k),), device_id_type=MESH)
+        return c
+
+    lax.fori_loop(1, N, greet, 0)
+
+    def fetch(r, c):
+        pltpu.make_async_copy(
+            state.at[:, :, pl.ds(pl.multiple_of(r * 128, 128), 128)],
+            tiles.at[pl.ds(r * 16, 16), pl.ds(0, 5), :],
+            load_sem,
+        ).start()
+        return c
+
+    lax.fori_loop(0, 32, fetch, 0)
+    bytes_of(tiles.at[:, pl.ds(0, 5), :], load_sem).wait()
+    rows = tiles.reshape(4096, 128)
+
+    def pack(m):
+        f = m // 32
+        r = lax.rem(m, 32)
+        return rows[pl.ds(r * 128 + f, 16, stride=8), :]
+
+    pl.semaphore_wait(barrier, N - 1)
+
+    def scatter(k, c):
+        m = partner(me, k)
+        send_a[m] = pack(m)
+        pltpu.make_async_remote_copy(
+            src_ref=send_a.at[m], dst_ref=recv_a.at[me], send_sem=send_sem.at[0], recv_sem=recv_sem.at[0],
+            device_id=(m,), device_id_type=MESH,
+        ).start()
+        return c
+
+    lax.fori_loop(1, N, scatter, 0)
+    recv_a[me] = pack(me)
+
+    def pack_rest(r, c):
+        tile = rows[pl.ds(r * 128 + 4, 16, stride=8), :]
+        for q in range(4):
+            send_ar[r * 4 + q] = jnp.concatenate(
+                [tile[4 * b:4 * b + 4, 32 * q:32 * q + 32] for b in range(4)], axis=1)
+        return c
+
+    lax.fori_loop(0, 32, pack_rest, 0)
+
+    def scatter_rest(k, c):
+        m = partner(me, k)
+        pltpu.make_async_remote_copy(
+            src_ref=send_ar.at[m], dst_ref=recv_ar.at[me], send_sem=send_sem.at[1], recv_sem=recv_sem.at[1],
+            device_id=(m,), device_id_type=MESH,
+        ).start()
+        return c
+
+    lax.fori_loop(1, N, scatter_rest, 0)
+    recv_ar[me] = send_ar[me]
+
+    wanted = new_map[...]
+
+    def find(s, c):
+        return jnp.where(wanted == old_map[s], s, c)
+
+    source = lax.fori_loop(0, 2048, find, jnp.zeros((16, 128), jnp.int32), unroll=8)
+    lane = lax.broadcasted_iota(jnp.int32, (16, 128), 1)
+    turn = (lane // 4 - source // 4 + 8) % 4
+    src_v[0:16] = source
+    src_v[16:32] = turn * 512 + source // 16 * 4 + source % 4
+    pltpu.make_async_copy(src_v, src_s, small_sem).start()
+    pltpu.make_async_copy(src_v, src_s, small_sem).wait()
+
+    bytes_of(recv_a.at[pl.ds(0, N - 1)], recv_sem.at[0]).wait()
+    bytes_of(recv_ar.at[pl.ds(0, N - 1)], recv_sem.at[1]).wait()
+
+    def turn_rest(s, c):
+        piece = recv_ar[pl.ds(s * 4, 4)].reshape(16, 128)
+        for t in range(4):
+            rolled[pl.ds(pl.multiple_of(t * 512 + s * 16, 16), 16), :] = (
+                pltpu.roll(piece, 32 * t, 1) if t else piece)
+        return c
+
+    lax.fori_loop(0, 32, turn_rest, 0)
+    arrived = recv_a.reshape(2048, 128)
+    quarter = lax.broadcasted_iota(jnp.int32, (1, 128), 1) // 32
+
+    def gather(d, into, into_rest):
+        hi = d // 8
+        lo = lax.rem(d, 8) * 16
+        for t in range(16):
+            into(t, arrived[pl.ds(src_s[hi, lo + t], 1), :])
+        for q in range(4):
+            row = jnp.zeros((1, 128), jnp.float32)
+            for i in range(4):
+                row = jnp.where(quarter == i, rolled[pl.ds(src_s[16 + hi, lo + i * 4 + q], 1), :], row)
+            into_rest(q, row)
+
+    def forward(k, c):
+        d = partner(me, k)
+
+        def into(t, row):
+            send_b[d, pl.ds(t, 1), :] = row
+
+        def into_rest(q, row):
+            send_br[d, pl.ds(q, 1), :] = row
+
+        gather(d, into, into_rest)
+        pltpu.make_async_remote_copy(
+            src_ref=send_b.at[d], dst_ref=cells.at[me], send_sem=send_sem.at[2], recv_sem=recv_sem.at[2],
+            device_id=(d,), device_id_type=MESH,
+        ).start()
+        pltpu.make_async_remote_copy(
+            src_ref=send_br.at[d], dst_ref=recv_br.at[me], send_sem=send_sem.at[3], recv_sem=recv_sem.at[3],
+            device_id=(d,), device_id_type=MESH,
+        ).start()
+        return c
+
+    lax.fori_loop(1, N, forward, 0)
+
+    def into_own(t, row):
+        cells[me, pl.ds(t, 1), :] = row
+
+    def into_own_rest(q, row):
+        recv_br[me, pl.ds(q, 1), :] = row
+
+    gather(me, into_own, into_own_rest)
+    bytes_of(cells.at[pl.ds(0, N - 1)], recv_sem.at[2]).wait()
+    bytes_of(recv_br.at[pl.ds(0, N - 1)], recv_sem.at[3]).wait()
+
+    def unpack_rest(r, c):
+        parts = [recv_br[r * 4 + q] for q in range(4)]
+        for b in range(4):
+            cells[128 + r, 4 * b:4 * b + 4, :] = jnp.concatenate(
+                [part[:, 32 * b:32 * b + 32] for part in parts], axis=1)
+        return c
+
+    lax.fori_loop(0, 32, unpack_rest, 0)
+    out[...] = cells[...]
+    for at, ref in ((0, send_a), (1, send_ar), (2, send_b), (3, send_br)):
+        bytes_of(ref.at[pl.ds(0, N - 1)], send_sem.at[at]).wait()
+
+
+def regrid(state, old_map, new_map):
+    vmem = pl.BlockSpec(memory_space=pltpu.VMEM)
+    f32 = jnp.float32
+    return pl.pallas_call(
+        kernel,
+        out_shape=jax.ShapeDtypeStruct((160, 16, 128), f32),
+        in_specs=[pl.BlockSpec(memory_space=pl.ANY), pl.BlockSpec(memory_space=pltpu.SMEM), vmem],
+        out_specs=vmem,
+        scratch_shapes=[
+            pltpu.VMEM((512, 8, 128), f32),
+            pltpu.VMEM((N, 16, 128), f32),
+            pltpu.VMEM((N, 4, 128), f32),
+            pltpu.VMEM((N, 16, 128), f32),
+            pltpu.VMEM((N, 4, 128), f32),
+            pltpu.VMEM((2048, 128), f32),
+            pltpu.VMEM((N, 16, 128), f32),
+            pltpu.VMEM((N, 4, 128), f32),
+            pltpu.VMEM((N, 4, 128), f32),
+            pltpu.VMEM((160, 16, 128), f32),
+            pltpu.VMEM((32, 128), jnp.int32),
+            pltpu.SMEM((32, 128), jnp.int32),
+            pltpu.SemaphoreType.DMA,
+            pltpu.SemaphoreType.DMA((4,)),
+            pltpu.SemaphoreType.DMA((4,)),
+            pltpu.SemaphoreType.DMA,
+        ],
+        compiler_params=pltpu.CompilerParams(
+            collective_id=0, has_side_effects=True, vmem_limit_bytes=48 << 20),
+    )(state, old_map, new_map.reshape(16, 128))
+
 
 E = 16
 GCAP = 20
@@ -113,39 +307,14 @@
     per_device, fields, volume = old_state.shape
     edge = E
     total = old_map.shape[0]
-    capacity = max(1, 2 * per_device // devices)
     plane_room = GCAP
     requests = 6 * per_device
     slots = jnp.arange(total, dtype=jnp.int32)
-    old_place = jnp.zeros((total,), jnp.int32).at[old_map].set(slots)
     new_place = jnp.zeros((total,), jnp.int32).at[new_map].set(slots)
-    target_device = (new_place[old_map] // per_device).reshape(devices, per_device)
-    counter = jnp.arange(per_device, dtype=jnp.int32)
-    earlier = counter[None, :] < counter[:, None]
-    send_rank = jnp.sum(
-        ((target_device[:, :, None] == target_device[:, None, :]) & earlier[None]).astype(
-            jnp.int32
-        ),
-        axis=2,
-    )
-    own_targets = lax.dynamic_index_in_dim(target_device, device_index, 0, False)
-    own_ranks = lax.dynamic_index_in_dim(send_rank, device_index, 0, False)
-    table = (
-        jnp.full((devices * capacity,), per_device, jnp.int32)
-        .at[own_targets * capacity + own_ranks]
-        .set(counter)
-    )
-    filled = table < per_device
-    picked = jnp.minimum(table, per_device - 1)
-    outgoing = jnp.where(filled[:, None, None], old_state[picked], 0.0).reshape(
-        devices, capacity, fields, volume
-    )
     own_boxes = lax.dynamic_slice_in_dim(new_map, device_index * per_device, per_device)
-    anchor = old_place[own_boxes]
-    position = anchor // per_device * capacity + send_rank.reshape(total)[anchor]
     own_scale = (2 - box_level[own_boxes]).astype(jnp.float32)
-    arrived = lax.all_to_all(outgoing, "boxes", split_axis=0, concat_axis=0, tiled=True)
-    regridded = arrived.reshape(-1, fields, volume)[position]
+    moved = regrid(old_state, old_map, new_map).reshape(fields, 32, per_device, 128)
+    regridded = moved.transpose(2, 0, 1, 3).reshape(per_device, fields, volume)
     cells = regridded.reshape(per_device, fields, edge, edge, edge)
     flat_cells = regridded.transpose(1, 0, 2).reshape(fields, per_device * volume)
     mine = requests_of(device_index, new_map, new_place, box_level, ghost_list, per_device)

time: 889 us -> 790 us (0.89)
  local copies, waits for them, and re-layouts: 502 us -> 423 us
  waiting for transfers between devices: 56.4 us -> 0.01 us
  Pallas kernels: 0 us -> 54.3 us
  other arithmetic: 35 us -> 23.9 us
  starting transfers between devices: 14.6 us -> 4.86 us
    reshape x5 -> x2, local copies, waits for them, and re-layouts: 59.7 us -> 2.97 us  [the longest x1 1.51 us: shards(): regridded = moved.transpose(2, 0, 1, 3).reshape(per_device, fields, volume)]
    all_to_all x1 -> x0, waiting for transfers between devices: 56.4 us -> none  [shards(): lax.all_to_all(outgoing, 'boxes', split_axis=0, concat_axis=0, tiled=True)]
    pallas_call x0 -> x1, Pallas kernels: none -> 54.3 us  [regrid(): pl.pallas_call(kernel, out_shape=jax.ShapeDtypeStruct((160, 16, 128), f32...]
    gather x7 -> x0, local copies, waits for them, and re-layouts: 38.9 us -> none  [the longest x1 19.2 us: shards(): old_state[picked]]
    another operation x1 -> x3, local copies, waits for them, and re-layouts: 0.09 us -> 22.8 us  [the longest x2 22.7 us: shards(): cells = regridded.reshape(per_device, fields, edge, edge, edge)]
    transpose x0 -> x2, local copies, waits for them, and re-layouts: none -> 16.6 us  [the longest x1 16.1 us: shards(): regridded.transpose(1, 0, 2).reshape(fields, per_device * volume)]
    select_n x1 -> x0, local copies, waits for them, and re-layouts: 13.2 us -> none  [shards(): jnp.where(filled[:, None, None], old_state[picked], 0.0)]
    all_to_all x1 -> x0, starting transfers between devices: 11.7 us -> none  [shards(): lax.all_to_all(outgoing, 'boxes', split_axis=0, concat_axis=0, tiled=True)]
  transfers between devices with their start and end apart: 5 -> 4, of which waited for: 1 -> 0; matrix products, arithmetic and copies ran while one was open for 36% -> 37% of each run, Pallas kernels for 0% -> 0%
where the time goes in v1:
time: 790 us; the launch traced here: 781 us
  local copies, waits for them, and re-layouts  423 us (54%)
  matrix products  273 us (35%)
  Pallas kernels  54.3 us (7%)
  other arithmetic  23.9 us (3%)
    dot_general x3, matrix products, mix_fields(): jnp.einsum('gf,fxyz->gxyz', matrix, field, precision=lax.Precision.HIGHEST)  273 us
    gather x5, local copies, waits for them, and re-layouts, planes_for(): taken = flat_cells[:, where_flat.reshape(-1)]  205 us
    pallas_call x1, Pallas kernels, regrid(): pl.pallas_call(kernel, out_shape=jax.ShapeDtypeStruct((160, 16, 128), f32...  54.3 us
    reshape x5, local copies, waits for them, and re-layouts, planes_for(): return taken.reshape(fields, count, edge, edge).transpose(1, 0, 2, 3)  28.1 us
    another operation x2, local copies, waits for them, and re-layouts, shards(): cells = regridded.reshape(per_device, fields, edge, edge, edge)  22.7 us
    transpose x1, local copies, waits for them, and re-layouts, shards(): regridded.transpose(1, 0, 2).reshape(fields, per_device * volume)  16.1 us
  transfers between devices with their start and end apart: 4, of which 0 were waited for; matrix products, arithmetic and copies ran while one was open for 37% of the time, Pallas kernels for 0%

profile of v1, /device:TPU:0, one launch (start us, length us, event | category | flops | bytes accessed | tf_op | source)
XLA Modules:
  0.0 780.6 jit_solution(10637213520862556728)
XLA Ops:
  2.3 4.3 copy.315
  7.3 2.8 gather_fusion.47
  10.2 2.8 gather_fusion.35
  14.5 8.0 %scatter_custom_fusion = s32[2048]{0:T(1024)S(1)} fusion(s32[2048]{0:T(1024)S(1)} %compare_select_fusion.13, s32[2048]{0:T(1024)S(1)} %iota.56, s32[]{:T(128)} %constant.210.clone.1), kind=kCustom, calls=%fused_computation.289 | custom fusion | bytes 8196 | tf_op jit(solution)/shard_map/scatter | solution.py:313
  26.0 54.3 %shard_map.64 = f32[160,16,128]{2,1,0:T(8,128)S(1)} custom-call(f32[16,5,4096]{2,1,0:T(8,128)S(1)} %copy.312.state, s32[2048]{0:T(1024)S(1)} %copy-done.3, s32[16,128]{1,0:T(8,128)S(1)} %bitcast.179), custom_call_target="tpu_custom_call" | custom-call | tf_op jit(solution)/shard_map/pallas_call | solution.py:172
  88.7 16.1 %copy.316 = f32[5,16,4096]{0,2,1:T(8,128)} copy(f32[5,16,4096]{2,1,0:T(8,128)S(1)} %bitcast.187) | data formatting | bytes 2621440 | tf_op jit(solution)/shard_map/transpose | solution.py:319
  104.9 28.2 %gather_fusion.57 = f32[5120,5]{1,0:T(8,128)} fusion(f32[5,65536]{0,1:T(8,128)} %bitcast.180, s32[5120]{0:T(1024)S(1)} %broadcast_clamp_fusion.1), kind=kCustom, calls=%fused_computation.57 | custom fusion | bytes 225280 | tf_op jit(solution)/shard_map/gather | solution.py:296
  133.0 3.8 copy.359
  137.3 3.1 collective-permute-start.3
  144.2 2.8 gather_fusion.23
  147.6 2.8 gather_fusion.11
  172.8 28.2 %gather_fusion.45 = f32[5120,5]{1,0:T(8,128)} fusion(f32[5,65536]{0,1:T(8,128)} %bitcast.181, s32[5120]{0:T(1024)S(1)} %broadcast_clamp_fusion.2), kind=kCustom, calls=%fused_computation.45 | custom fusion | bytes 225280 | tf_op jit(solution)/shard_map/gather | solution.py:296
  201.0 3.8 copy.350
  208.9 28.2 %gather_fusion.33 = f32[5120,5]{1,0:T(8,128)} fusion(f32[5,65536]{0,1:T(8,128)} %bitcast.182, s32[5120]{0:T(1024)S(1)} %broadcast_clamp_fusion.3), kind=kCustom, calls=%fused_computation.33 | custom fusion | bytes 225280 | tf_op jit(solution)/shard_map/gather | solution.py:296
  237.1 3.8 copy.341
  247.1 28.2 %gather_fusion.21 = f32[5120,5]{1,0:T(8,128)} fusion(f32[5,65536]{0,1:T(8,128)} %bitcast.183, s32[5120]{0:T(1024)S(1)} %broadcast_clamp_fusion.4), kind=kCustom, calls=%fused_computation.21 | custom fusion | bytes 225280 | tf_op jit(solution)/shard_map/gather | solution.py:296
  275.3 3.8 copy.328
  281.4 2.8 gather_fusion.1
  299.9 5.9 reshape_reshape.3
  305.8 16.8 %copy.377 = f32[16,5,16,16,16]{4,1,3,2,0:T(8,128)} copy(f32[16,5,16,16,16]{4,3,2,1,0:T(8,128)} %reshape_reshape.3) | data formatting | bytes 2621440 | tf_op jit(solution)/shard_map/reshape;reshape | solution.py:318
  322.6 91.8 %gather_fusion.10 = f32[24576,5]{1,0:T(8,128)} fusion(f32[5,65536]{0,1:T(8,128)} %bitcast.184, s32[24576]{0:T(1024)S(1)} %broadcast_clamp_fusion), kind=kCustom, calls=%fused_computation.10 | custom fusion | bytes 1081344 | tf_op jit(solution)/shard_map/gather | solution.py:296
  414.5 13.1 %copy.321 = f32[5,96,16,16]{3,2,0,1:T(8,128)} copy(f32[5,96,16,16]{0,3,2,1:T(8,128)} %bitcast.186) | data formatting | bytes 983040 | tf_op jit(solution)/shard_map/reshape | solution.py:297
  435.8 3.8 gather_fusion.22
  445.1 2.8 gather_fusion.58
  447.9 7.7 fusion.11
  460.7 11.3 %copy.365 = f32[16,5,16,16,1]{4,1,3,2,0:T(8,128)} copy(f32[16,5,16,16,1]{3,2,1,0,4:T(8,128)} %get-tuple-element.41) | data formatting | bytes 163840 | tf_op jit(solution)/shard_map/vmap()/broadcast_in_dim;vmap()/squeeze | solution.py:240
  472.0 10.4 %copy.363 = f32[16,5,16,16,1]{4,1,3,2,0:T(8,128)} copy(f32[16,5,16,16,1]{3,2,1,0,4:T(8,128)S(1)} %copy-done.4) | data formatting | bytes 163840 | tf_op jit(solution)/shard_map/vmap()/broadcast_in_dim;vmap()/squeeze | solution.py:240
  484.8 36.4 %fusion.1 = f32[16,16,16,16,5]{3,4,2,1,0:T(8,128)} fusion(f32[16,5,16,16,1]{4,1,3,2,0:T(8,128)} %copy.365, f32[16,5,16,16,16]{4,1,3,2,0:T(8,128)} %copy.377, f32[16,5,16,16,1]{4,1,3,2,0:T(8,128)} %copy.363, f32[1,5,5]{2,0,1:T(1,128)S(1)} %copy-done.9), kind=kOutput, calls=%fused_computation.84 | convolution fusion | flops 20643840 | bytes 2785380 | tf_op jit(solution)/shard_map/vmap(gf,fxyz->gxyz)/dot_general | solution.py:215
  521.3 38.7 %fusion.3 = f32[16,16,16,16,5]{3,4,2,1,0:T(8,128)} fusion(f32[1,5,5]{2,0,1:T(1,128)S(1)} %copy-done.18, f32[16,5,16,1,18]{4,1,3,2,0:T(8,128)} %get-tuple-element.44, f32[16,5,16,16,1]{4,1,3,2,0:T(8,128)} %copy.365, f32[16,5,16,16,16]{4,1,3,2,0:T(8,128)} %copy.377, f32[16,5,16,16,1]{4,1,3,2,0:T(8,128)} %copy.363, f32[16,5,16,1,18]{4,1,3,2,0:T(8,128)S(1)} %copy-done.8), kind=kOutput, calls=%fused_computation.86 | convolution fusion | flops 21954560 | bytes 2969700 | tf_op jit(solution)/shard_map/vmap(gf,fxyz->gxyz)/dot_general | solution.py:215
  560.1 197.9 %fusion = f32[16,5,16,16,16]{4,1,3,2,0:T(8,128)} fusion(f32[16,5,16,16,16]{4,1,3,2,0:T(8,128)} %copy.377, f32[16,16,16,16,5]{3,4,2,1,0:T(8,128)} %fusion.1, f32[16,16,16,16,5]{3,4,2,1,0:T(8,128)} %fusion.3, f32[16,5,1,18,18]{4,1,3,2,0:T(8,128)S(1)} %copy-done.7, f32[16,5,16,1,18]{4,1,3,2,0:T(8,128)} %get-tuple-element.44, f32[16,5,16,16,1]{4,1,3,2,0:T(8,128)} %copy.365, ...), kind=kOutput, calls=%fused_computation.83 | convolution fusion | flops 33423360 | bytes 5798628 | tf_op jit(solution)/shard_map/vmap(gf,fxyz->gxyz)/dot_general | solution.py:215
  758.0 11.8 %copy.378 = f32[16,5,16,16,16]{4,3,2,0,1:T(8,128)} copy(f32[16,5,16,16,16]{4,1,3,2,0:T(8,128)} %fusion) | data formatting | bytes 2621440 | tf_op jit(solution)/shard_map/vmap()/add | solution.py:252
  769.8 10.3 %reshape.1799 = f32[16,5,4096]{2,0,1:T(8,128)} reshape(f32[16,5,16,16,16]{4,3,2,0,1:T(8,128)} %copy.378) | data formatting | bytes 2621440 | tf_op jit(solution)/shard_map/reshape | solution.py:347
  (303 shorter events, 92.3 us)
Async XLA Ops:
  0.0 6.7 copy-start
  0.0 25.9 %copy-start.2 = (s32[2048]{0:T(1024)S(1)}, s32[2048]{0:T(1024)}, u32[]{:S(2)}) copy-start(s32[2048]{0:T(1024)} %param.12) | copy-start | bytes 24580
  0.0 25.1 %copy-start.5 = (f32[16,5,4096]{2,0,1:T(8,128)S(1)}, f32[16,5,4096]{2,0,1:T(8,128)}, u32[]{:S(2)}) copy-start(f32[16,5,4096]{2,0,1:T(8,128)} %param.10) | copy-start | bytes 3932164
  0.0 25.9 %copy-start.3 = (s32[2048]{0:T(1024)S(1)}, s32[2048]{0:T(1024)}, u32[]{:S(2)}) copy-start(s32[2048]{0:T(1024)} %old_map.1) | copy-start | bytes 24580
  0.1 171.2 %copy-start.13 = (s32[16]{0:T(128)}, s32[16]{0:T(128)S(1)}, u32[]{:S(2)}) copy-start(s32[16]{0:T(128)S(1)} %sign_bitcast_fusion) | copy-start | bytes 196
  137.3 290.3 %collective-permute-start.3 = (f32[20,5,256]{2,0,1:T(8,128)S(1)}, f32[20,5,256]{2,0,1:T(8,128)S(1)}, u32[]{:S(2)}, u32[]{:S(2)}) collective-permute-start(f32[20,5,256]{2,0,1:T(8,128)S(1)} %reshape.1796), channel_id=1, source_target_pairs={{0,126},{1,127},{2,0},{3,1},{4,2},{5,3},{6,4},{7,5},{8,6},{9,7},{1... | collective-permute-start | bytes 307208 | tf_op jit(solution)/shard_map/ppermute | solution.py:211
  160.0 2.9 copy-start.22
  160.0 2.9 copy-start.11
  160.7 44.0 %copy-start.16 = (s32[20]{0:T(128)}, s32[20]{0:T(128)S(1)}, u32[]{:S(2)}) copy-start(s32[20]{0:T(128)S(1)} %gather_fusion.27) | copy-start | bytes 244
  164.2 0.7 copy-start.21
  164.2 7.1 copy-start.10
  164.9 39.9 %copy-start.15 = (s32[20]{0:T(128)}, s32[20]{0:T(128)S(1)}, u32[]{:S(2)}) copy-start(s32[20]{0:T(128)S(1)} %gather_fusion.15) | copy-start | bytes 244
  205.3 222.6 %collective-permute-start.2 = (f32[20,5,256]{2,0,1:T(8,128)S(1)}, f32[20,5,256]{2,0,1:T(8,128)S(1)}, u32[]{:S(2)}, u32[]{:S(2)}) collective-permute-start(f32[20,5,256]{2,0,1:T(8,128)S(1)} %reshape.1793), channel_id=1, source_target_pairs={{0,127},{1,0},{2,1},{3,2},{4,3},{5,4},{6,5},{7,6},{8,7},{9,8},{10,... | collective-permute-start | bytes 307208 | tf_op jit(solution)/shard_map/ppermute | solution.py:211
  237.1 51.7 %copy-start.12 = (f32[3,5,5]{2,0,1:T(4,128)S(1)}, f32[3,5,5]{2,0,1:T(4,128)}, u32[]{:S(2)}) copy-start(f32[3,5,5]{2,0,1:T(4,128)} %param.15) | copy-start | bytes 904
  241.0 55.7 %copy-start.14 = (s32[16]{0:T(128)S(1)}, s32[16]{0:T(128)}, u32[]{:S(2)}) copy-start(s32[16]{0:T(128)} %copy-done.13) | copy-start | bytes 196
  242.0 186.3 %collective-permute-start.1 = (f32[20,5,256]{2,0,1:T(8,128)}, f32[20,5,256]{2,0,1:T(8,128)}, u32[]{:S(2)}, u32[]{:S(2)}) collective-permute-start(f32[20,5,256]{2,0,1:T(8,128)} %reshape.1790), channel_id=1, source_target_pairs={{0,2},{1,3},{2,4},{3,5},{4,6},{5,7},{6,8},{7,9},{8,10},{9,11},{10,... | collective-permute-start | bytes 307208 | tf_op jit(solution)/shard_map/ppermute | solution.py:211
  280.2 151.4 %collective-permute-start = (f32[20,5,256]{2,0,1:T(8,128)}, f32[20,5,256]{2,0,1:T(8,128)}, u32[]{:S(2)}, u32[]{:S(2)}) collective-permute-start(f32[20,5,256]{2,0,1:T(8,128)} %reshape.1787), channel_id=1, source_target_pairs={{0,1},{1,2},{2,3},{3,4},{4,5},{5,6},{6,7},{7,8},{8,9},{9,10},{10,1... | collective-permute-start | bytes 307208 | tf_op jit(solution)/shard_map/ppermute | solution.py:211
  460.1 11.9 %copy-start.4 = (f32[16,5,16,16,1]{3,2,1,0,4:T(8,128)S(1)}, f32[16,5,16,16,1]{3,2,1,0,4:T(8,128)}, u32[]{:S(2)}) copy-start(f32[16,5,16,16,1]{3,2,1,0,4:T(8,128)} %get-tuple-element.42) | copy-start | bytes 245764
  460.7 24.1 %copy-start.9 = (f32[1,5,5]{2,0,1:T(1,128)S(1)}, f32[1,5,5]{2,0,1:T(1,128)}, u32[]{:S(2)}) copy-start(f32[1,5,5]{2,0,1:T(1,128)} %get-tuple-element.51) | copy-start | bytes 304
  484.8 36.4 %copy-start.8 = (f32[16,5,16,1,18]{4,1,3,2,0:T(8,128)S(1)}, f32[16,5,16,1,18]{4,1,3,2,0:T(8,128)}, u32[]{:S(2)}) copy-start(f32[16,5,16,1,18]{4,1,3,2,0:T(8,128)} %get-tuple-element.43) | copy-start | bytes 276484
  484.8 36.4 %copy-start.18 = (f32[1,5,5]{2,0,1:T(1,128)S(1)}, f32[1,5,5]{2,0,1:T(1,128)}, u32[]{:S(2)}) copy-start(f32[1,5,5]{2,0,1:T(1,128)} %get-tuple-element.50) | copy-start | bytes 304
  521.2 38.8 %copy-start.6 = (f32[16,5,1,18,18]{4,1,3,2,0:T(8,128)S(1)}, f32[16,5,1,18,18]{4,1,3,2,0:T(8,128)}, u32[]{:S(2)}) copy-start(f32[16,5,1,18,18]{4,1,3,2,0:T(8,128)} %pad_bitcast_fusion) | copy-start | bytes 311044
  521.2 38.8 %copy-start.7 = (f32[16,5,1,18,18]{4,1,3,2,0:T(8,128)S(1)}, f32[16,5,1,18,18]{4,1,3,2,0:T(8,128)}, u32[]{:S(2)}) copy-start(f32[16,5,1,18,18]{4,1,3,2,0:T(8,128)} %pad_bitcast_fusion.1) | copy-start | bytes 311044
  521.3 38.8 %copy-start.17 = (f32[1,5,5]{2,0,1:T(1,128)S(1)}, f32[1,5,5]{2,0,1:T(1,128)}, u32[]{:S(2)}) copy-start(f32[1,5,5]{2,0,1:T(1,128)} %get-tuple-element.49) | copy-start | bytes 304
  521.3 38.8 %copy-start.19 = (f32[16]{0:T(128)S(1)}, f32[16]{0:T(128)}, u32[]{:S(2)}) copy-start(f32[16]{0:T(128)} %get-tuple-element.81) | copy-start | bytes 196
  521.3 38.8 %copy-start.20 = (f32[16]{0:T(128)S(1)}, f32[16]{0:T(128)}, u32[]{:S(2)}) copy-start(f32[16]{0:T(128)} %get-tuple-element.82) | copy-start | bytes 196
  560.1 220.1 %copy-start.1 = (s32[2048]{0:T(1024)S(1)}, s32[2048]{0:T(1024)}, u32[]{:S(2)}) copy-start(s32[2048]{0:T(1024)} %param.13) | copy-start | bytes 24580

commit v2 on v1

v2 whole, which is shorter than its diff:
```python
import functools

import jax
import jax.numpy as jnp
from jax import lax
from jax.experimental import pallas as pl
from jax.experimental.pallas import tpu as pltpu
from jax.sharding import PartitionSpec as P

MESH = pl.DeviceIdType.MESH
N = 128
BOXES = 16
STRIDE = 37
DISTANCES = (-2, -1, 1, 2)
ROOM = 20
ROWS = 24
PITCH = 36
BLOCK = 10 * BOXES
diffusion_number = 0.12
advection_number = 0.25


def partner(me, k):
    return lax.rem(me + k * STRIDE, N)


def bytes_of(ref, sem):
    return pltpu.make_async_copy(ref, ref, sem)


def put(src, dst, send_sem, recv_sem, device):
    pltpu.make_async_remote_copy(
        src_ref=src, dst_ref=dst, send_sem=send_sem, recv_sem=recv_sem, device_id=(device,), device_id_type=MESH,
    ).start()


def iota(shape, axis):
    return lax.broadcasted_iota(jnp.int32, shape, axis)


def running_count(chosen):
    lane = iota(chosen.shape, 1)
    count = chosen.astype(jnp.int32)
    for step in (1, 2, 4, 8, 16, 32, 64):
        count = count + jnp.where(lane >= step, pltpu.roll(count, step, 1), 0)
    return count


def swap_bits(rows, unit, steps):
    lane = iota(rows[0].shape, 1)
    rows = list(rows)
    for step in steps:
        high = (lane // (unit * step)) % 2 == 1
        for at in range(len(rows)):
            if at & step:
                continue
            low_row, high_row = rows[at], rows[at + step]
            rows[at] = jnp.where(high, pltpu.roll(high_row, unit * step, 1), low_row)
            rows[at + step] = jnp.where(high, high_row, pltpu.roll(low_row, 128 - unit * step, 1))
    return rows


def kernel(state, old_map, new_map, new_lanes, box_level, ghost_list, coupling, out,
           rest, send_ar, recv_a, recv_ar, rolled, send_b, send_br, recv_br, cells, src_v, src_s,
           old_s, new_s, level_s, ghost_s, mix_s, new_v, face_code, level_v, table_v, table_s,
           planes, outbox, inbox, raw, raw_far, faces,
           load_sem, send_sem, recv_sem, small_sem, far_send, far_recv):
    me = lax.axis_index("boxes")
    barrier = pltpu.get_barrier_semaphore()

    def greet(k, c):
        pl.semaphore_signal(barrier, inc=1, device_id=(partner(me, k),), device_id_type=MESH)
        return c

    lax.fori_loop(1, N, greet, 0)
    loads = [
        pltpu.make_async_copy(state.at[4], rest, load_sem.at[0]),
        pltpu.make_async_copy(old_map, old_s, load_sem.at[1]),
        pltpu.make_async_copy(new_map, new_s, load_sem.at[2]),
        pltpu.make_async_copy(new_lanes, new_v, load_sem.at[3]),
        pltpu.make_async_copy(box_level, level_s, load_sem.at[4]),
        pltpu.make_async_copy(ghost_list, ghost_s, load_sem.at[5]),
        pltpu.make_async_copy(coupling, mix_s, load_sem.at[6]),
    ]
    for load in loads:
        load.start()

    def piece(m):
        return state.at[m // 32, :, pl.ds(pl.multiple_of(lax.rem(m, 32) * 128, 128), 128)]

    own = pltpu.make_async_copy(piece(me), recv_a.at[me], load_sem.at[7])
    own.start()
    pl.semaphore_wait(barrier, N - 1)

    def scatter(k, c):
        m = partner(me, k)
        put(piece(m), recv_a.at[me], send_sem.at[0], recv_sem.at[0], m)
        return c

    lax.fori_loop(1, N, scatter, 0)
    loads[0].wait()

    def pack_rest(r, c):
        tile = rest[:, pl.ds(pl.multiple_of(r * 128, 128), 128)]
        for q in range(4):
            send_ar[r * 4 + q] = jnp.concatenate(
                [tile[4 * b:4 * b + 4, 32 * q:32 * q + 32] for b in range(4)], axis=1)
        return c

    lax.fori_loop(0, 32, pack_rest, 0)

    def scatter_rest(k, c):
        m = partner(me, k)
        put(send_ar.at[m], recv_ar.at[me], send_sem.at[1], recv_sem.at[1], m)
        return c

    lax.fori_loop(1, N, scatter_rest, 0)
    recv_ar[me] = send_ar[me]
    for load in loads[1:]:
        load.wait()

    wanted = new_v[...]

    def find(s, c):
        return jnp.where(wanted == old_s[s], s, c)

    source = lax.fori_loop(0, 2048, find, jnp.zeros((16, 128), jnp.int32), unroll=8)
    lane = iota((16, 128), 1)
    turn = (lane // 4 - source // 4 + 8) % 4
    src_v[0:16] = source
    src_v[16:32] = turn * 512 + source // 16 * 4 + source % 4
    to_scalars = pltpu.make_async_copy(src_v, src_s, small_sem.at[0])
    to_scalars.start()

    row8, lane8 = iota((8, 128), 0), iota((8, 128), 1)
    row16 = iota((16, 128), 0)
    nothing = jnp.full((8, 128), -1, jnp.int32)
    zeros16 = jnp.zeros((16, 128), jnp.int32)

    def read_wishes(k, c):
        theirs, their_plane, ours, our_plane, level_here, codes = c
        for at, distance in enumerate(DISTANCES):
            b = new_s[lax.rem(me + distance + N, N) * BOXES + k]
            for f in range(6):
                here = (row8 == at) & (lane8 == f * 16 + k)
                theirs = jnp.where(here, ghost_s[f, 0, b], theirs)
                their_plane = jnp.where(here, ghost_s[f, 1, b], their_plane)
        b = new_s[me * BOXES + k]
        level = level_s[b]
        level_here = jnp.where(row16 == k, level, level_here)
        new_codes = []
        for f in range(6):
            here = lane8 == f * 16 + k
            g = ghost_s[f, 0, b]
            ours = jnp.where(here, g, ours)
            our_plane = jnp.where(here, ghost_s[f, 1, b], our_plane)
            coarser = (level_s[jnp.maximum(g, 0)] < level).astype(jnp.int32)
            code = ghost_s[f, 2, b] // 8 + ghost_s[f, 3, b] // 8 * 2 + coarser * 4
            new_codes.append(jnp.where(row16 == k, code, codes[f]))
        return theirs, their_plane, ours, our_plane, level_here, tuple(new_codes)

    theirs, their_plane, ours, our_plane, level_here, codes = lax.fori_loop(
        0, BOXES, read_wishes, (nothing, nothing, nothing, nothing, zeros16, (zeros16,) * 6))
    level_v[...] = level_here
    for f in range(6):
        face_code[f] = codes[f]

    def find_theirs(t, c):
        return jnp.where(theirs == new_s[me * BOXES + t], t, c)

    their_slot = lax.fori_loop(0, BOXES, find_theirs, nothing)

    def find_ours(t, c):
        return jnp.where(ours == new_s[lax.rem((me - 2 + N) * BOXES + t, N * BOXES)], t, c)

    our_slot = lax.fori_loop(0, 5 * BOXES, find_ours, nothing)
    axis = lane8 // 32
    chosen = their_slot >= 0
    count = running_count(chosen)
    base = (axis * 16 + their_plane) * BLOCK + their_slot
    table = jnp.zeros((8, 128), jnp.int32)
    for j in range(ROOM):
        first = jnp.sum(jnp.where(chosen & (count == j + 1), base, 0), axis=1, keepdims=True)
        table = jnp.where(lane8 == j, first, table)
    low = jnp.where(row8 == 4, 32, jnp.where(row8 >= 2, row8 * 16 + 16, row8 * 16))
    chosen = (our_slot >= low) & (our_slot < low + 16) & (row8 < 5)
    count = running_count(chosen)
    far_base = jnp.sum(
        jnp.where(chosen & (row8 < 4), row8 * (10 * ROWS) + count - 1 - 40 * ROWS, 0), axis=0, keepdims=True)
    near_base = jnp.sum(
        jnp.where(chosen & (row8 == 4), (axis * 16 + our_plane) * BLOCK + our_slot - 32 - 48 * BLOCK, 0),
        axis=0, keepdims=True)
    table = jnp.where(row8 == 4, far_base + 40 * ROWS, table)
    table = jnp.where(row8 == 5, near_base + 48 * BLOCK, table)
    table_v[...] = table
    to_table = pltpu.make_async_copy(table_v, table_s, small_sem.at[1])
    to_table.start()
    planes[48] = jnp.zeros((10, BOXES, 128), jnp.float32)
    inbox[4] = jnp.zeros((10, ROWS, 128), jnp.float32)
    to_scalars.wait()
    to_table.wait()

    own.wait()
    bytes_of(recv_a.at[pl.ds(0, N - 1)], recv_sem.at[0]).wait()
    bytes_of(recv_ar.at[pl.ds(0, N - 1)], recv_sem.at[1]).wait()

    def turn_rest(s, c):
        part = recv_ar[pl.ds(s * 4, 4)].reshape(16, 128)
        for t in range(4):
            rolled[pl.ds(pl.multiple_of(t * 512 + s * 16, 16), 16), :] = (
                pltpu.roll(part, 32 * t, 1) if t else part)
        return c

    lax.fori_loop(0, 32, turn_rest, 0)
    arrived = recv_a.reshape(2048, 128)
    quarter = iota((1, 128), 1) // 32
    landing = me // 32 * PITCH + 2 + lax.rem(me, 32)

    def gather(d, into, into_rest):
        hi = d // 8
        lo = lax.rem(d, 8) * 16
        for t in range(16):
            into(t, arrived[pl.ds(src_s[hi, lo + t], 1), :])
        for q in range(4):
            row = jnp.zeros((1, 128), jnp.float32)
            for i in range(4):
                row = jnp.where(quarter == i, rolled[pl.ds(src_s[16 + hi, lo + i * 4 + q], 1), :], row)
            into_rest(q, row)

    def forward(k, c):
        d = partner(me, k)

        def into(t, row):
            send_b[d, pl.ds(t, 1), :] = row

        def into_rest(q, row):
            send_br[d, pl.ds(q, 1), :] = row

        gather(d, into, into_rest)
        put(send_b.at[d], cells.at[landing], send_sem.at[2], recv_sem.at[2], d)
        put(send_br.at[d], recv_br.at[me], send_sem.at[3], recv_sem.at[3], d)
        return c

    lax.fori_loop(1, N, forward, 0)

    def into_own(t, row):
        cells[landing, pl.ds(t, 1), :] = row

    def into_own_rest(q, row):
        recv_br[me, pl.ds(q, 1), :] = row

    gather(me, into_own, into_own_rest)
    bytes_of(cells.at[pl.ds(0, N - 1)], recv_sem.at[2]).wait()
    bytes_of(recv_br.at[pl.ds(0, N - 1)], recv_sem.at[3]).wait()

    def unpack_rest(r, c):
        parts = [recv_br[r * 4 + q] for q in range(4)]
        for b in range(4):
            cells[4 * PITCH + 2 + r, 4 * b:4 * b + 4, :] = jnp.concatenate(
                [part[:, 32 * b:32 * b + 32] for part in parts], axis=1)
        return c

    lax.fori_loop(0, 32, unpack_rest, 0)

    def transpose_planes(at, c):
        f, half, b = at // 4, at // 2 % 2, pl.multiple_of(at % 2 * 8, 8)
        rows = [cells[f * PITCH + 2 + 2 * i + half, pl.ds(b, 8), :] for i in range(16)]
        for i in range(16):
            planes[i, 2 * f + half, pl.ds(b, 8), :] = rows[i]
        for upper in range(2):
            turned = swap_bits(rows[8 * upper:8 * upper + 8], 16, (4, 2, 1))
            for j in range(8):
                planes[16 + 8 * half + j, 2 * f + upper, pl.ds(b, 8), :] = turned[j]
        turned = swap_bits(rows, 1, (8, 4, 2, 1))
        for k in range(16):
            planes[32 + k, 2 * f + half, pl.ds(b, 8), :] = turned[k]
        return c

    lax.fori_loop(0, 20, transpose_planes, 0)
    plane_rows = planes.reshape(49 * BLOCK, 128)

    for at, distance in enumerate(DISTANCES):
        def fill(j, c, at=at):
            base = table_s[at, j]
            for h in range(10):
                outbox[at, h, pl.ds(j, 1), :] = plane_rows[pl.ds(base + h * BOXES, 1), :]
            return c

        lax.fori_loop(0, ROOM, fill, 0)
        put(outbox.at[at], inbox.at[3 - at], far_send.at[at], far_recv.at[3 - at],
            lax.rem(me + distance + N, N))

    def take_near(q, c):
        base = table_s[5, q]
        for h in range(10):
            raw[h, pl.ds(q, 1), :] = plane_rows[pl.ds(base + h * BOXES, 1), :]
        return c

    lax.fori_loop(0, 96, take_near, 0)
    for at in range(4):
        bytes_of(inbox.at[at], far_recv.at[at]).wait()
    inbox_rows = inbox.reshape(50 * ROWS, 128)

    def take_far(q, c):
        base = table_s[4, q]
        for h in range(10):
            raw_far[h, pl.ds(q, 1), :] = inbox_rows[pl.ds(base + h * ROWS, 1), :]
        return c

    lax.fori_loop(0, 96, take_far, 0)

    lane = iota((16, 128), 1)
    for face in range(6):
        code = face_code[face]
        coarse = code >= 4
        first, second = code % 2, code // 2 % 2
        if face >= 4:
            first, second = second, first
        picks = [
            jnp.where(coarse, (4 * half + lane // 32) * 16 + 8 * second + lane % 16 // 2, lane)
            for half in range(2)
        ]
        low_first = coarse & (first == 0)
        high_first = coarse & (first == 1)

        def refine(f, c, face=face, picks=picks, low_first=low_first, high_first=high_first):
            part = [raw[2 * f + h, 16 * face:16 * face + 16, :] + raw_far[2 * f + h, 16 * face:16 * face + 16, :]
                    for h in range(2)]
            chosen = [jnp.where(high_first, part[1], part[0]), jnp.where(low_first, part[0], part[1])]
            for h in range(2):
                value = jnp.take_along_axis(chosen[h], picks[h], axis=1, mode="promise_in_bounds")
                if face < 2:
                    cells[f * PITCH + 34 * face + h] = value
                else:
                    faces[face - 2, 2 * f + h] = value
            return c

        lax.fori_loop(0, 5, refine, 0)

    lane = iota((8, 128), 1)
    third = lane % 16

    def step(at, c):
        i, b = at // 2, pl.multiple_of(at % 2 * 8, 8)
        eighth = lax.rem(i, 8)
        scale = (2 - level_v[pl.ds(b, 8), :]).astype(jnp.float32)
        spread = diffusion_number / (scale * scale)
        drift = advection_number / scale * 0.5

        def at_row(f, r):
            return cells[f * PITCH + 2 + r, pl.ds(b, 8), :]

        values = [[at_row(f, 2 * i + h) for h in range(2)] for f in range(5)]
        for half in range(2):
            sums, differences = [], []
            for f in range(5):
                here, other = values[f][half], values[f][1 - half]
                before, after = at_row(f, 2 * i + half - 2), at_row(f, 2 * i + half + 2)
                total = after + before - 6.0 * here
                moves = [after - before]
                if half == 0:
                    edge = pltpu.roll(
                        faces[0, 2 * f + i // 8, pl.ds(b, 8), :], lax.rem(128 - eighth * 16, 128), 1)
                    before = jnp.where(lane < 16, edge, pltpu.roll(here, 16, 1))
                    after = pltpu.roll(jnp.where(lane < 16, other, here), 112, 1)
                else:
                    edge = pltpu.roll(faces[1, 2 * f + i // 8, pl.ds(b, 8), :], 112 - eighth * 16, 1)
                    before = pltpu.roll(jnp.where(lane >= 112, other, here), 16, 1)
                    after = jnp.where(lane >= 112, edge, pltpu.roll(here, 112, 1))
                total = total + (after + before)
                moves.append(after - before)
                edge = pltpu.roll(faces[2, 2 * f + half, pl.ds(b, 8), :], lax.rem(128 - i, 128), 1)
                before = jnp.where(third == 0, edge, pltpu.roll(here, 1, 1))
                edge = pltpu.roll(faces[3, 2 * f + half, pl.ds(b, 8), :], 15 - i, 1)
                after = jnp.where(third == 15, edge, pltpu.roll(here, 127, 1))
                total = total + (after + before)
                moves.append(after - before)
                sums.append(total)
                differences.append(moves)
            for g in range(5):
                flux = None
                for a in range(3):
                    for f in range(5):
                        term = mix_s[a, g, f] * differences[f][a]
                        flux = term if flux is None else flux + term
                value = values[g][half] + (spread * sums[g] - drift * flux)
                out[g, pl.ds(b, 8), pl.ds(pl.multiple_of((2 * i + half) * 128, 128), 128)] = value
        return c

    lax.fori_loop(0, 32, step, 0)
    bytes_of(recv_a.at[pl.ds(0, N - 1)], send_sem.at[0]).wait()
    for at, ref in ((1, send_ar), (2, send_b), (3, send_br)):
        bytes_of(ref.at[pl.ds(0, N - 1)], send_sem.at[at]).wait()
    for at in range(4):
        bytes_of(outbox.at[at], far_send.at[at]).wait()


def shards(old_state, old_map, new_map, box_level, ghost_list, coupling):
    vmem = pl.BlockSpec(memory_space=pltpu.VMEM)
    anywhere = pl.BlockSpec(memory_space=pl.ANY)
    f32, i32 = jnp.float32, jnp.int32
    dma = pltpu.SemaphoreType.DMA
    stepped = pl.pallas_call(
        kernel,
        out_shape=jax.ShapeDtypeStruct((5, BOXES, 4096), f32),
        in_specs=[anywhere] * 7,
        out_specs=vmem,
        scratch_shapes=[
            pltpu.VMEM((BOXES, 4096), f32),
            pltpu.VMEM((N, 4, 128), f32),
            pltpu.VMEM((N, BOXES, 128), f32),
            pltpu.VMEM((N, 4, 128), f32),
            pltpu.VMEM((2048, 128), f32),
            pltpu.VMEM((N, BOXES, 128), f32),
            pltpu.VMEM((N, 4, 128), f32),
            pltpu.VMEM((N, 4, 128), f32),
            pltpu.VMEM((5 * PITCH, BOXES, 128), f32),
            pltpu.VMEM((32, 128), i32),
            pltpu.SMEM((32, 128), i32),
            pltpu.SMEM((2048,), i32),
            pltpu.SMEM((2048,), i32),
            pltpu.SMEM((2048,), i32),
            pltpu.SMEM((6, 4, 2048), i32),
            pltpu.SMEM((3, 5, 5), f32),
            pltpu.VMEM((16, 128), i32),
            pltpu.VMEM((6, 16, 128), i32),
            pltpu.VMEM((16, 128), i32),
            pltpu.VMEM((8, 128), i32),
            pltpu.SMEM((8, 128), i32),
            pltpu.VMEM((49, 10, BOXES, 128), f32),
            pltpu.VMEM((4, 10, ROWS, 128), f32),
            pltpu.VMEM((5, 10, ROWS, 128), f32),
            pltpu.VMEM((10, 96, 128), f32),
            pltpu.VMEM((10, 96, 128), f32),
            pltpu.VMEM((4, 10, BOXES, 128), f32),
            dma((8,)),
            dma((4,)),
            dma((4,)),
            dma((2,)),
            dma((4,)),
            dma((4,)),
        ],
        compiler_params=pltpu.CompilerParams(
            collective_id=0, has_side_effects=True, vmem_limit_bytes=48 << 20),
    )(
        old_state.transpose(1, 0, 2), old_map, new_map, new_map.reshape(16, 128), box_level,
        ghost_list.transpose(1, 2, 0), coupling,
    )
    return stepped.transpose(1, 0, 2)


def solution(mesh):
    return jax.shard_map(
        shards,
        mesh=mesh,
        in_specs=(P("boxes", None, None), P(), P(), P(), P(), P()),
        out_specs=P("boxes", None, None),
        check_vma=False,
    )
```

time: 790 us -> 83.2 us (0.11); the launches traced: 781 us -> 81.9 us
  local copies, waits for them, and re-layouts: 423 us -> 6.09 us
  matrix products: 273 us -> 0 us
  other arithmetic: 23.9 us -> 0 us
  Pallas kernels: 54.3 us -> 75.8 us
    dot_general x3 -> x0, matrix products: 273 us -> none  [mix_fields(): jnp.einsum('gf,fxyz->gxyz', matrix, field, precision=lax.Precision.HIGHEST)]
    gather x69 -> x0, local copies, waits for them, and re-layouts: 271 us -> none  [the longest x5 205 us: planes_for(): taken = flat_cells[:, where_flat.reshape(-1)]]
    reshape x21 -> x0, local copies, waits for them, and re-layouts: 52.4 us -> none  [the longest x5 28.1 us: planes_for(): return taken.reshape(fields, count, edge, edge).transpose(1, 0, 2, 3)]
    another operation x18 -> x0, local copies, waits for them, and re-layouts: 24.1 us -> none  [the longest x2 22.7 us: shards(): cells = regridded.reshape(per_device, fields, edge, edge, edge)]
    squeeze x2 -> x0, local copies, waits for them, and re-layouts: 21.8 us -> none  [the longest x1 11.3 us: surround(): ghosts[5][:, :, :, None]]
    pallas_call x1, Pallas kernels: 54.3 us -> 75.8 us  [shards(): pl.pallas_call(kernel, out_shape=jax.ShapeDtypeStruct((5, BOXES, 4096), f...]
    transpose x2 -> x0, local copies, waits for them, and re-layouts: 16.6 us -> none  [the longest x1 16.1 us: shards(): regridded.transpose(1, 0, 2).reshape(fields, per_device * volume)]
    add x7 -> x0, local copies, waits for them, and re-layouts: 12.6 us -> none  [the longest x1 11.8 us: stencil_step(): return cells + increment_from(padded, cells, scale, coupling)]
  transfers between devices with their start and end apart: 4 -> 0, of which waited for: 0 -> 0; matrix products, arithmetic and copies ran while one was open for 37% -> 0% of each run, Pallas kernels for 0% -> 0%
where the time goes in v2:
time: 83.2 us; the launch traced here: 81.9 us
  Pallas kernels  75.8 us (91%)
  local copies, waits for them, and re-layouts  6.09 us (7%)
    pallas_call x1, Pallas kernels, shards(): pl.pallas_call(kernel, out_shape=jax.ShapeDtypeStruct((5, BOXES, 4096), f...  75.8 us
    unnamed x12, local copies, waits for them, and re-layouts  6.09 us

profile of v2, /device:TPU:0, one launch (start us, length us, event | category | flops | bytes accessed | tf_op | source)
XLA Modules:
  0.0 81.9 jit_solution(14146989894339121478)
XLA Ops:
  0.0 0.7 copy.7.coupling
  0.7 0.0 copy-start
  0.7 1.3 %copy-done = f32[16,5,4096]{2,0,1:T(8,128)S(1)} copy-done((f32[16,5,4096]{2,0,1:T(8,128)S(1)}, f32[16,5,4096]{2,0,1:T(8,128)}, u32[]{:S(2)}) %copy-start) | copy-done | bytes 1310744
  2.0 0.0 copy-start.1
  2.0 0.9 %copy-done.1 = s32[2048,6,4]{0,2,1:T(4,128)S(1)} copy-done((s32[2048,6,4]{0,2,1:T(4,128)S(1)}, s32[2048,6,4]{0,2,1:T(4,128)}, u32[]{:S(2)}) %copy-start.1) | copy-done | bytes 196632
  2.9 0.0 copy-start.2
  3.0 0.7 copy-done.2
  3.6 0.0 copy-start.3
  3.6 0.7 copy-done.3
  4.3 0.0 copy-start.4
  4.3 0.7 copy-done.4
  5.0 75.8 %shard_map.64 = f32[5,16,4096]{2,1,0:T(8,128)S(1)} custom-call(f32[5,16,4096]{2,1,0:T(8,128)S(1)} %bitcast.5, s32[2048]{0:T(1024)S(1)} %copy-done.3, s32[2048]{0:T(1024)S(1)} %copy-done.2, s32[16,128]{1,0:T(8,128)S(1)} %bitcast.7, s32[2048]{0:T(1024)S(1)} %copy-done.4, s32[6,4,2048]{2,1,0:T(4,128)S(1)} %bitcast.6, f32[3,5,5]{2,1,0:T(8,128)S(1)} %copy.7.coupling), custom_call_target="tpu_custom_call" | custom-call | tf_op jit(solution)/shard_map/pallas_call | solution.py:403
  80.8 1.1 %copy.9 = f32[16,5,4096]{2,0,1:T(8,128)} copy(f32[16,5,4096]{2,0,1:T(8,128)S(1)} %bitcast.4) | data formatting | bytes 2621440
Async XLA Ops:
  0.7 1.3 %copy-start = (f32[16,5,4096]{2,0,1:T(8,128)S(1)}, f32[16,5,4096]{2,0,1:T(8,128)}, u32[]{:S(2)}) copy-start(f32[16,5,4096]{2,0,1:T(8,128)} %param.6) | copy-start | bytes 3932164
  2.0 0.9 %copy-start.1 = (s32[2048,6,4]{0,2,1:T(4,128)S(1)}, s32[2048,6,4]{0,2,1:T(4,128)}, u32[]{:S(2)}) copy-start(s32[2048,6,4]{0,2,1:T(4,128)} %param.10) | copy-start | bytes 589828
  2.9 0.7 copy-start.2
  3.6 0.7 copy-start.3
  4.3 0.7 copy-start.4

commit v3 on v2

--- a/solution.py
+++ b/solution.py
@@ -1,5 +1,3 @@
-import functools
-
 import jax
 import jax.numpy as jnp
 from jax import lax
@@ -11,7 +9,7 @@
 N = 128
 BOXES = 16
 STRIDE = 37
-DISTANCES = (-2, -1, 1, 2)
+DISTANCES = (-2, 2, -1, 1)
 ROOM = 20
 ROWS = 24
 PITCH = 36
@@ -50,7 +48,7 @@
     lane = iota(rows[0].shape, 1)
     rows = list(rows)
     for step in steps:
-        high = (lane // (unit * step)) % 2 == 1
+        high = (lane & (unit * step)) != 0
         for at in range(len(rows)):
             if at & step:
                 continue
@@ -182,7 +180,9 @@
     for j in range(ROOM):
         first = jnp.sum(jnp.where(chosen & (count == j + 1), base, 0), axis=1, keepdims=True)
         table = jnp.where(lane8 == j, first, table)
-    low = jnp.where(row8 == 4, 32, jnp.where(row8 >= 2, row8 * 16 + 16, row8 * 16))
+    low = jnp.where(row8 == 4, 32, 0)
+    for at, distance in enumerate(DISTANCES):
+        low = jnp.where(row8 == at, 16 * (distance + 2), low)
     chosen = (our_slot >= low) & (our_slot < low + 16) & (row8 < 5)
     count = running_count(chosen)
     far_base = jnp.sum(
@@ -197,11 +197,31 @@
     to_table.start()
     planes[48] = jnp.zeros((10, BOXES, 128), jnp.float32)
     inbox[4] = jnp.zeros((10, ROWS, 128), jnp.float32)
+    for f in range(5):
+        for edge in (0, 1, 34, 35):
+            cells[f * PITCH + edge] = jnp.zeros((BOXES, 128), jnp.float32)
     to_scalars.wait()
     to_table.wait()
 
     own.wait()
     bytes_of(recv_a.at[pl.ds(0, N - 1)], recv_sem.at[0]).wait()
+    arrived = recv_a.reshape(2048, 128)
+    landing = me // 32 * PITCH + 2 + lax.rem(me, 32)
+
+    def gather(d, into):
+        hi = d // 8
+        lo = lax.rem(d, 8) * 16
+        for t in range(16):
+            into[pl.ds(t, 1), :] = arrived[pl.ds(src_s[hi, lo + t], 1), :]
+
+    def forward(k, c):
+        d = partner(me, k)
+        gather(d, send_b.at[d])
+        put(send_b.at[d], cells.at[landing], send_sem.at[2], recv_sem.at[2], d)
+        return c
+
+    lax.fori_loop(1, N, forward, 0)
+    gather(me, cells.at[landing])
     bytes_of(recv_ar.at[pl.ds(0, N - 1)], recv_sem.at[1]).wait()
 
     def turn_rest(s, c):
@@ -212,58 +232,28 @@
         return c
 
     lax.fori_loop(0, 32, turn_rest, 0)
-    arrived = recv_a.reshape(2048, 128)
-    quarter = iota((1, 128), 1) // 32
-    landing = me // 32 * PITCH + 2 + lax.rem(me, 32)
-
-    def gather(d, into, into_rest):
-        hi = d // 8
+    lane1 = iota((1, 128), 1)
+
+    def gather_rest(d, into):
+        hi = 16 + d // 8
         lo = lax.rem(d, 8) * 16
-        for t in range(16):
-            into(t, arrived[pl.ds(src_s[hi, lo + t], 1), :])
         for q in range(4):
-            row = jnp.zeros((1, 128), jnp.float32)
-            for i in range(4):
-                row = jnp.where(quarter == i, rolled[pl.ds(src_s[16 + hi, lo + i * 4 + q], 1), :], row)
-            into_rest(q, row)
-
-    def forward(k, c):
+            part = [rolled[pl.ds(src_s[hi, lo + i * 4 + q], 1), :] for i in range(4)]
+            into[pl.ds(q, 1), :] = jnp.where(
+                lane1 < 64, jnp.where(lane1 < 32, part[0], part[1]), jnp.where(lane1 < 96, part[2], part[3]))
+
+    def forward_rest(k, c):
         d = partner(me, k)
-
-        def into(t, row):
-            send_b[d, pl.ds(t, 1), :] = row
-
-        def into_rest(q, row):
-            send_br[d, pl.ds(q, 1), :] = row
-
-        gather(d, into, into_rest)
-        put(send_b.at[d], cells.at[landing], send_sem.at[2], recv_sem.at[2], d)
+        gather_rest(d, send_br.at[d])
         put(send_br.at[d], recv_br.at[me], send_sem.at[3], recv_sem.at[3], d)
         return c
 
-    lax.fori_loop(1, N, forward, 0)
-
-    def into_own(t, row):
-        cells[landing, pl.ds(t, 1), :] = row
-
-    def into_own_rest(q, row):
-        recv_br[me, pl.ds(q, 1), :] = row
-
-    gather(me, into_own, into_own_rest)
+    lax.fori_loop(1, N, forward_rest, 0)
+    gather_rest(me, recv_br.at[me])
     bytes_of(cells.at[pl.ds(0, N - 1)], recv_sem.at[2]).wait()
-    bytes_of(recv_br.at[pl.ds(0, N - 1)], recv_sem.at[3]).wait()
-
-    def unpack_rest(r, c):
-        parts = [recv_br[r * 4 + q] for q in range(4)]
-        for b in range(4):
-            cells[4 * PITCH + 2 + r, 4 * b:4 * b + 4, :] = jnp.concatenate(
-                [part[:, 32 * b:32 * b + 32] for part in parts], axis=1)
-        return c
-
-    lax.fori_loop(0, 32, unpack_rest, 0)
 
     def transpose_planes(at, c):
-        f, half, b = at // 4, at // 2 % 2, pl.multiple_of(at % 2 * 8, 8)
+        f, half, b = at >> 2, (at >> 1) & 1, pl.multiple_of((at & 1) * 8, 8)
         rows = [cells[f * PITCH + 2 + 2 * i + half, pl.ds(b, 8), :] for i in range(16)]
         for i in range(16):
             planes[i, 2 * f + half, pl.ds(b, 8), :] = rows[i]
@@ -276,7 +266,17 @@
             planes[32 + k, 2 * f + half, pl.ds(b, 8), :] = turned[k]
         return c
 
-    lax.fori_loop(0, 20, transpose_planes, 0)
+    lax.fori_loop(0, 16, transpose_planes, 0)
+    bytes_of(recv_br.at[pl.ds(0, N - 1)], recv_sem.at[3]).wait()
+
+    def unpack_rest(r, c):
+        parts = [recv_br[pl.ds(r * 32 + q, 8, stride=4)].reshape(32, 128) for q in range(4)]
+        for b, part in enumerate(swap_bits(parts, 32, (2, 1))):
+            cells[pl.ds(4 * PITCH + 2 + 8 * r, 8), 4 * b:4 * b + 4, :] = part.reshape(8, 4, 128)
+        return c
+
+    lax.fori_loop(0, 4, unpack_rest, 0)
+    lax.fori_loop(16, 20, transpose_planes, 0)
     plane_rows = planes.reshape(49 * BLOCK, 128)
 
     for at, distance in enumerate(DISTANCES):
@@ -286,8 +286,8 @@
                 outbox[at, h, pl.ds(j, 1), :] = plane_rows[pl.ds(base + h * BOXES, 1), :]
             return c
 
-        lax.fori_loop(0, ROOM, fill, 0)
-        put(outbox.at[at], inbox.at[3 - at], far_send.at[at], far_recv.at[3 - at],
+        lax.fori_loop(0, ROOM, fill, 0, unroll=4)
+        put(outbox.at[at], inbox.at[at ^ 1], far_send.at[at], far_recv.at[at ^ 1],
             lax.rem(me + distance + N, N))
 
     def take_near(q, c):
@@ -296,56 +296,18 @@
             raw[h, pl.ds(q, 1), :] = plane_rows[pl.ds(base + h * BOXES, 1), :]
         return c
 
-    lax.fori_loop(0, 96, take_near, 0)
-    for at in range(4):
-        bytes_of(inbox.at[at], far_recv.at[at]).wait()
-    inbox_rows = inbox.reshape(50 * ROWS, 128)
-
-    def take_far(q, c):
-        base = table_s[4, q]
-        for h in range(10):
-            raw_far[h, pl.ds(q, 1), :] = inbox_rows[pl.ds(base + h * ROWS, 1), :]
-        return c
-
-    lax.fori_loop(0, 96, take_far, 0)
-
-    lane = iota((16, 128), 1)
-    for face in range(6):
-        code = face_code[face]
-        coarse = code >= 4
-        first, second = code % 2, code // 2 % 2
-        if face >= 4:
-            first, second = second, first
-        picks = [
-            jnp.where(coarse, (4 * half + lane // 32) * 16 + 8 * second + lane % 16 // 2, lane)
-            for half in range(2)
-        ]
-        low_first = coarse & (first == 0)
-        high_first = coarse & (first == 1)
-
-        def refine(f, c, face=face, picks=picks, low_first=low_first, high_first=high_first):
-            part = [raw[2 * f + h, 16 * face:16 * face + 16, :] + raw_far[2 * f + h, 16 * face:16 * face + 16, :]
-                    for h in range(2)]
-            chosen = [jnp.where(high_first, part[1], part[0]), jnp.where(low_first, part[0], part[1])]
-            for h in range(2):
-                value = jnp.take_along_axis(chosen[h], picks[h], axis=1, mode="promise_in_bounds")
-                if face < 2:
-                    cells[f * PITCH + 34 * face + h] = value
-                else:
-                    faces[face - 2, 2 * f + h] = value
-            return c
-
-        lax.fori_loop(0, 5, refine, 0)
+    lax.fori_loop(0, 96, take_near, 0, unroll=4)
 
     lane = iota((8, 128), 1)
-    third = lane % 16
+    third = lane & 15
+
+    def factors(b):
+        scale = (2 - level_v[pl.ds(b, 8), :]).astype(jnp.float32)
+        return diffusion_number / (scale * scale), advection_number / scale * 0.5
 
     def step(at, c):
-        i, b = at // 2, pl.multiple_of(at % 2 * 8, 8)
-        eighth = lax.rem(i, 8)
-        scale = (2 - level_v[pl.ds(b, 8), :]).astype(jnp.float32)
-        spread = diffusion_number / (scale * scale)
-        drift = advection_number / scale * 0.5
+        i, b = at >> 1, pl.multiple_of((at & 1) * 8, 8)
+        spread, drift = factors(b)
 
         def at_row(f, r):
             return cells[f * PITCH + 2 + r, pl.ds(b, 8), :]
@@ -359,20 +321,15 @@
                 total = after + before - 6.0 * here
                 moves = [after - before]
                 if half == 0:
-                    edge = pltpu.roll(
-                        faces[0, 2 * f + i // 8, pl.ds(b, 8), :], lax.rem(128 - eighth * 16, 128), 1)
-                    before = jnp.where(lane < 16, edge, pltpu.roll(here, 16, 1))
+                    before = jnp.where(lane < 16, 0.0, pltpu.roll(here, 16, 1))
                     after = pltpu.roll(jnp.where(lane < 16, other, here), 112, 1)
                 else:
-                    edge = pltpu.roll(faces[1, 2 * f + i // 8, pl.ds(b, 8), :], 112 - eighth * 16, 1)
                     before = pltpu.roll(jnp.where(lane >= 112, other, here), 16, 1)
-                    after = jnp.where(lane >= 112, edge, pltpu.roll(here, 112, 1))
+                    after = jnp.where(lane >= 112, 0.0, pltpu.roll(here, 112, 1))
                 total = total + (after + before)
                 moves.append(after - before)
-                edge = pltpu.roll(faces[2, 2 * f + half, pl.ds(b, 8), :], lax.rem(128 - i, 128), 1)
-                before = jnp.where(third == 0, edge, pltpu.roll(here, 1, 1))
-                edge = pltpu.roll(faces[3, 2 * f + half, pl.ds(b, 8), :], 15 - i, 1)
-                after = jnp.where(third == 15, edge, pltpu.roll(here, 127, 1))
+                before = jnp.where(third == 0, 0.0, pltpu.roll(here, 1, 1))
+                after = jnp.where(third == 15, 0.0, pltpu.roll(here, 127, 1))
                 total = total + (after + before)
                 moves.append(after - before)
                 sums.append(total)
@@ -381,13 +338,85 @@
                 flux = None
                 for a in range(3):
                     for f in range(5):
-                        term = mix_s[a, g, f] * differences[f][a]
+                        term = mix_s[g, a, f] * differences[f][a]
                         flux = term if flux is None else flux + term
                 value = values[g][half] + (spread * sums[g] - drift * flux)
                 out[g, pl.ds(b, 8), pl.ds(pl.multiple_of((2 * i + half) * 128, 128), 128)] = value
         return c
 
     lax.fori_loop(0, 32, step, 0)
+
+    for at in range(4):
+        bytes_of(inbox.at[at], far_recv.at[at]).wait()
+    inbox_rows = inbox.reshape(50 * ROWS, 128)
+
+    def take_far(q, c):
+        base = table_s[4, q]
+        for h in range(10):
+            raw_far[h, pl.ds(q, 1), :] = inbox_rows[pl.ds(base + h * ROWS, 1), :]
+        return c
+
+    lax.fori_loop(0, 96, take_far, 0, unroll=4)
+
+    for face in range(6):
+        def add_face(part, c, face=face):
+            b = pl.multiple_of(part * 8, 8)
+            spread, drift = factors(b)
+            code = face_code[face, pl.ds(b, 8), :]
+            coarse = code >= 4
+            first, second = code & 1, (code >> 1) & 1
+            if face >= 4:
+                first, second = second, first
+            low_first = coarse & (first == 0)
+            high_first = coarse & (first == 1)
+            fine_pick = ((lane >> 5) << 4) + second * 8 + ((lane & 15) >> 1)
+            picks = [jnp.where(coarse, 64 * half + fine_pick, lane) for half in range(2)]
+            ghost = []
+            for f in range(5):
+                rows = pl.ds(16 * face + b, 8)
+                half = [raw[2 * f + h, rows, :] + raw_far[2 * f + h, rows, :] for h in range(2)]
+                chosen = [jnp.where(high_first, half[1], half[0]), jnp.where(low_first, half[0], half[1])]
+                ghost.append([
+                    jnp.take_along_axis(chosen[h], picks[h], axis=1, mode="promise_in_bounds")
+                    for h in range(2)])
+            for g in range(5):
+                for h in range(2):
+                    flux = None
+                    for f in range(5):
+                        term = mix_s[g, face // 2, f] * ghost[f][h]
+                        flux = term if flux is None else flux + term
+                    sign = drift if face % 2 == 0 else -drift
+                    value = spread * ghost[g][h] + sign * flux
+                    if face < 2:
+                        at = (30 * face + h) * 128
+                        out[g, pl.ds(b, 8), at:at + 128] = out[g, pl.ds(b, 8), at:at + 128] + value
+                    else:
+                        faces[face - 2, 2 * g + h, pl.ds(b, 8), :] = value
+            return c
+
+        lax.fori_loop(0, 2, add_face, 0)
+
+    def spread_faces(at, c):
+        i, b = at >> 1, pl.multiple_of((at & 1) * 8, 8)
+        eighth = (i & 7) * 16
+        upper = i >> 3
+        for g in range(5):
+            for half in range(2):
+                cut = pl.ds(pl.multiple_of((2 * i + half) * 128, 128), 128)
+                lower_third = pltpu.roll(faces[2, 2 * g + half, pl.ds(b, 8), :], (128 - i) & 127, 1)
+                upper_third = pltpu.roll(faces[3, 2 * g + half, pl.ds(b, 8), :], 15 - i, 1)
+                value = out[g, pl.ds(b, 8), cut] + jnp.where(
+                    third == 0, lower_third, jnp.where(third == 15, upper_third, 0.0))
+                if half == 0:
+                    edge = pltpu.roll(faces[0, 2 * g + upper, pl.ds(b, 8), :], (128 - eighth) & 127, 1)
+                    value = value + jnp.where(lane < 16, edge, 0.0)
+                else:
+                    edge = pltpu.roll(faces[1, 2 * g + upper, pl.ds(b, 8), :], 112 - eighth, 1)
+                    value = value + jnp.where(lane >= 112, edge, 0.0)
+                out[g, pl.ds(b, 8), cut] = value
+        return c
+
+    lax.fori_loop(0, 32, spread_faces, 0)
     bytes_of(recv_a.at[pl.ds(0, N - 1)], send_sem.at[0]).wait()
     for at, ref in ((1, send_ar), (2, send_b), (3, send_br)):
         bytes_of(ref.at[pl.ds(0, N - 1)], send_sem.at[at]).wait()
@@ -397,13 +426,13 @@
 
 def shards(old_state, old_map, new_map, box_level, ghost_list, coupling):
     vmem = pl.BlockSpec(memory_space=pltpu.VMEM)
-    anywhere = pl.BlockSpec(memory_space=pl.ANY)
+    hbm = pl.BlockSpec(memory_space=pltpu.HBM)
     f32, i32 = jnp.float32, jnp.int32
     dma = pltpu.SemaphoreType.DMA
     stepped = pl.pallas_call(
         kernel,
         out_shape=jax.ShapeDtypeStruct((5, BOXES, 4096), f32),
-        in_specs=[anywhere] * 7,
+        in_specs=[hbm] * 7,
         out_specs=vmem,
         scratch_shapes=[
             pltpu.VMEM((BOXES, 4096), f32),
@@ -421,7 +450,7 @@
             pltpu.SMEM((2048,), i32),
             pltpu.SMEM((2048,), i32),
             pltpu.SMEM((6, 4, 2048), i32),
-            pltpu.SMEM((3, 5, 5), f32),
+            pltpu.SMEM((5, 3, 5), f32),
             pltpu.VMEM((16, 128), i32),
             pltpu.VMEM((6, 16, 128), i32),
             pltpu.VMEM((16, 128), i32),
@@ -444,7 +473,7 @@
             collective_id=0, has_side_effects=True, vmem_limit_bytes=48 << 20),
     )(
         old_state.transpose(1, 0, 2), old_map, new_map, new_map.reshape(16, 128), box_level,
-        ghost_list.transpose(1, 2, 0), coupling,
+        ghost_list.transpose(1, 2, 0), coupling.transpose(1, 0, 2),
     )
     return stepped.transpose(1, 0, 2)
 

time: 83.2 us -> 70 us (0.84); the launches traced: 81.9 us -> 69.7 us
  Pallas kernels: 75.8 us -> 63.6 us
    pallas_call x1, Pallas kernels: 75.8 us -> 63.6 us  [shards(): pl.pallas_call(kernel, out_shape=jax.ShapeDtypeStruct((5, BOXES, 4096), f...]
    unnamed x12 -> x13, local copies, waits for them, and re-layouts: 6.09 us -> 6.09 us
where the time goes in v3:
time: 70 us; the launch traced here: 69.7 us
  Pallas kernels  63.6 us (91%)
  local copies, waits for them, and re-layouts  6.09 us (9%)
    pallas_call x1, Pallas kernels, shards(): pl.pallas_call(kernel, out_shape=jax.ShapeDtypeStruct((5, BOXES, 4096), f...  63.6 us
    unnamed x13, local copies, waits for them, and re-layouts  6.09 us

profile of v3, /device:TPU:0, one launch (start us, length us, event | category | flops | bytes accessed | tf_op | source)
XLA Modules:
  0.0 69.7 jit_solution(17398913356107126197)
XLA Ops:
  0.0 0.0 copy-start
  0.0 1.3 %copy-done = f32[16,5,4096]{2,0,1:T(8,128)S(1)} copy-done((f32[16,5,4096]{2,0,1:T(8,128)S(1)}, f32[16,5,4096]{2,0,1:T(8,128)}, u32[]{:S(2)}) %copy-start) | copy-done | bytes 1310744
  1.3 0.0 copy-start.1
  1.3 0.9 %copy-done.1 = s32[2048,6,4]{0,2,1:T(4,128)S(1)} copy-done((s32[2048,6,4]{0,2,1:T(4,128)S(1)}, s32[2048,6,4]{0,2,1:T(4,128)}, u32[]{:S(2)}) %copy-start.1) | copy-done | bytes 196632
  2.2 0.0 copy-start.2
  2.2 0.7 copy-done.2
  2.9 0.0 copy-start.3
  2.9 0.7 %copy-done.3 = f32[3,5,5]{2,0,1:T(4,128)S(1)} copy-done((f32[3,5,5]{2,0,1:T(4,128)S(1)}, f32[3,5,5]{2,0,1:T(4,128)}, u32[]{:S(2)}) %copy-start.3) | copy-done | bytes 324
  3.6 0.0 copy-start.4
  3.6 0.7 copy-done.4
  4.3 0.0 copy-start.5
  4.3 0.7 copy-done.5
  5.0 63.6 %shard_map.64 = f32[5,16,4096]{2,1,0:T(8,128)S(1)} custom-call(f32[5,16,4096]{2,1,0:T(8,128)S(1)} %bitcast.6, s32[2048]{0:T(1024)S(1)} %copy-done.4, s32[2048]{0:T(1024)S(1)} %copy-done.2, s32[16,128]{1,0:T(8,128)S(1)} %bitcast.8, s32[2048]{0:T(1024)S(1)} %copy-done.5, s32[6,4,2048]{2,1,0:T(4,128)S(1)} %bitcast.7, f32[5,3,5]{2,1,0:T(4,128)S(1)} %bitcast.9), custom_call_target="tpu_custom_call" | custom-call | tf_op jit(solution)/shard_map/pallas_call | solution.py:432
  68.6 1.1 %copy.8 = f32[16,5,4096]{2,0,1:T(8,128)} copy(f32[16,5,4096]{2,0,1:T(8,128)S(1)} %bitcast.5) | data formatting | bytes 2621440
Async XLA Ops:
  0.0 1.3 %copy-start = (f32[16,5,4096]{2,0,1:T(8,128)S(1)}, f32[16,5,4096]{2,0,1:T(8,128)}, u32[]{:S(2)}) copy-start(f32[16,5,4096]{2,0,1:T(8,128)} %param.6) | copy-start | bytes 3932164
  1.3 0.9 %copy-start.1 = (s32[2048,6,4]{0,2,1:T(4,128)S(1)}, s32[2048,6,4]{0,2,1:T(4,128)}, u32[]{:S(2)}) copy-start(s32[2048,6,4]{0,2,1:T(4,128)} %param.10) | copy-start | bytes 589828
  2.2 0.7 copy-start.2
  2.9 0.7 %copy-start.3 = (f32[3,5,5]{2,0,1:T(4,128)S(1)}, f32[3,5,5]{2,0,1:T(4,128)}, u32[]{:S(2)}) copy-start(f32[3,5,5]{2,0,1:T(4,128)} %param.11) | copy-start | bytes 904
  3.6 0.7 copy-start.4
  4.3 0.7 copy-start.5

commit v4 on v3

--- a/solution.py
+++ b/solution.py
@@ -8,12 +8,13 @@
 MESH = pl.DeviceIdType.MESH
 N = 128
 BOXES = 16
-STRIDE = 37
+STRIDE = 27
 DISTANCES = (-2, 2, -1, 1)
 ROOM = 20
 ROWS = 24
 PITCH = 36
 BLOCK = 10 * BOXES
+EARLY = 24
 diffusion_number = 0.12
 advection_number = 0.25
 
@@ -53,15 +54,20 @@
             if at & step:
                 continue
             low_row, high_row = rows[at], rows[at + step]
-            rows[at] = jnp.where(high, pltpu.roll(high_row, unit * step, 1), low_row)
-            rows[at + step] = jnp.where(high, high_row, pltpu.roll(low_row, 128 - unit * step, 1))
+            crossed = jnp.where(high, low_row, high_row)
+            if unit * step == 64:
+                crossed = pltpu.roll(crossed, 64, 1)
+            else:
+                crossed = jnp.take_along_axis(crossed, lane ^ (unit * step), axis=1, mode="promise_in_bounds")
+            rows[at] = jnp.where(high, crossed, low_row)
+            rows[at + step] = jnp.where(high, high_row, crossed)
     return rows
 
 
 def kernel(state, old_map, new_map, new_lanes, box_level, ghost_list, coupling, out,
            rest, send_ar, recv_a, recv_ar, rolled, send_b, send_br, recv_br, cells, src_v, src_s,
            old_s, new_s, level_s, ghost_s, mix_s, new_v, face_code, level_v, table_v, table_s,
-           planes, outbox, inbox, raw, raw_far, faces,
+           planes, outbox, inbox, inbox_last, raw, raw_far, faces,
            load_sem, send_sem, recv_sem, small_sem, far_send, far_recv):
     me = lax.axis_index("boxes")
     barrier = pltpu.get_barrier_semaphore()
@@ -185,18 +191,21 @@
         low = jnp.where(row8 == at, 16 * (distance + 2), low)
     chosen = (our_slot >= low) & (our_slot < low + 16) & (row8 < 5)
     count = running_count(chosen)
-    far_base = jnp.sum(
-        jnp.where(chosen & (row8 < 4), row8 * (10 * ROWS) + count - 1 - 40 * ROWS, 0), axis=0, keepdims=True)
+    for row, count_of in ((4, 8), (6, 2)):
+        pitch = count_of * ROWS
+        far_base = jnp.sum(
+            jnp.where(chosen & (row8 < 4), row8 * pitch + count - 1 - 4 * pitch, 0), axis=0, keepdims=True)
+        table = jnp.where(row8 == row, far_base + 4 * pitch, table)
     near_base = jnp.sum(
         jnp.where(chosen & (row8 == 4), (axis * 16 + our_plane) * BLOCK + our_slot - 32 - 48 * BLOCK, 0),
         axis=0, keepdims=True)
-    table = jnp.where(row8 == 4, far_base + 40 * ROWS, table)
     table = jnp.where(row8 == 5, near_base + 48 * BLOCK, table)
     table_v[...] = table
     to_table = pltpu.make_async_copy(table_v, table_s, small_sem.at[1])
     to_table.start()
     planes[48] = jnp.zeros((10, BOXES, 128), jnp.float32)
-    inbox[4] = jnp.zeros((10, ROWS, 128), jnp.float32)
+    inbox[4] = jnp.zeros((8, ROWS, 128), jnp.float32)
+    inbox_last[4] = jnp.zeros((2, ROWS, 128), jnp.float32)
     for f in range(5):
         for edge in (0, 1, 34, 35):
             cells[f * PITCH + edge] = jnp.zeros((BOXES, 128), jnp.float32)
@@ -266,37 +275,29 @@
             planes[32 + k, 2 * f + half, pl.ds(b, 8), :] = turned[k]
         return c
 
-    lax.fori_loop(0, 16, transpose_planes, 0)
-    bytes_of(recv_br.at[pl.ds(0, N - 1)], recv_sem.at[3]).wait()
-
-    def unpack_rest(r, c):
-        parts = [recv_br[pl.ds(r * 32 + q, 8, stride=4)].reshape(32, 128) for q in range(4)]
-        for b, part in enumerate(swap_bits(parts, 32, (2, 1))):
-            cells[pl.ds(4 * PITCH + 2 + 8 * r, 8), 4 * b:4 * b + 4, :] = part.reshape(8, 4, 128)
-        return c
-
-    lax.fori_loop(0, 4, unpack_rest, 0)
-    lax.fori_loop(16, 20, transpose_planes, 0)
     plane_rows = planes.reshape(49 * BLOCK, 128)
 
-    for at, distance in enumerate(DISTANCES):
-        def fill(j, c, at=at):
-            base = table_s[at, j]
-            for h in range(10):
-                outbox[at, h, pl.ds(j, 1), :] = plane_rows[pl.ds(base + h * BOXES, 1), :]
+    def send_planes(first, count, part):
+        cut = pl.ds(first, count)
+        for at, distance in enumerate(DISTANCES):
+            def fill(j, c, at=at):
+                base = table_s[at, j]
+                for h in range(first, first + count):
+                    outbox[at, h, pl.ds(j, 1), :] = plane_rows[pl.ds(base + h * BOXES, 1), :]
+                return c
+
+            lax.fori_loop(0, ROOM, fill, 0, unroll=4)
+            put(outbox.at[at, cut], (inbox, inbox_last)[part].at[at ^ 1], far_send.at[part, at], far_recv.at[part, at ^ 1],
+                lax.rem(me + distance + N, N))
+
+    def take_near(first, count):
+        def take(q, c):
+            base = table_s[5, q]
+            for h in range(first, first + count):
+                raw[h, pl.ds(q, 1), :] = plane_rows[pl.ds(base + h * BOXES, 1), :]
             return c
 
-        lax.fori_loop(0, ROOM, fill, 0, unroll=4)
-        put(outbox.at[at], inbox.at[at ^ 1], far_send.at[at], far_recv.at[at ^ 1],
-            lax.rem(me + distance + N, N))
-
-    def take_near(q, c):
-        base = table_s[5, q]
-        for h in range(10):
-            raw[h, pl.ds(q, 1), :] = plane_rows[pl.ds(base + h * BOXES, 1), :]
-        return c
-
-    lax.fori_loop(0, 96, take_near, 0, unroll=4)
+        lax.fori_loop(0, 96, take, 0, unroll=4)
 
     lane = iota((8, 128), 1)
     third = lane & 15
@@ -305,17 +306,17 @@
         scale = (2 - level_v[pl.ds(b, 8), :]).astype(jnp.float32)
         return diffusion_number / (scale * scale), advection_number / scale * 0.5
 
-    def step(at, c):
+    def step(at, fields):
         i, b = at >> 1, pl.multiple_of((at & 1) * 8, 8)
         spread, drift = factors(b)
 
         def at_row(f, r):
             return cells[f * PITCH + 2 + r, pl.ds(b, 8), :]
 
-        values = [[at_row(f, 2 * i + h) for h in range(2)] for f in range(5)]
+        values = {f: [at_row(f, 2 * i + h) for h in range(2)] for f in fields}
         for half in range(2):
-            sums, differences = [], []
-            for f in range(5):
+            sums, differences = {}, {}
+            for f in fields:
                 here, other = values[f][half], values[f][1 - half]
                 before, after = at_row(f, 2 * i + half - 2), at_row(f, 2 * i + half + 2)
                 total = after + before - 6.0 * here
@@ -332,96 +333,134 @@
                 after = jnp.where(third == 15, 0.0, pltpu.roll(here, 127, 1))
                 total = total + (after + before)
                 moves.append(after - before)
-                sums.append(total)
-                differences.append(moves)
+                sums[f] = total
+                differences[f] = [drift * move for move in moves]
             for g in range(5):
+                value = None
+                if 0 not in fields:
+                    value = out[g, pl.ds(b, 8), pl.ds(pl.multiple_of((2 * i + half) * 128, 128), 128)]
+                if g in fields:
+                    own = values[g][half] + spread * sums[g]
+                    value = own if value is None else value + own
+                for a in range(3):
+                    for f in fields:
+                        term = mix_s[g, a, f] * differences[f][a]
+                        value = -term if value is None else value - term
+                out[g, pl.ds(b, 8), pl.ds(pl.multiple_of((2 * i + half) * 128, 128), 128)] = value
+
+    def step_four(at, c):
+        step(at, (0, 1, 2, 3))
+        return c
+
+    def step_last(at, c):
+        step(at, (4,))
+        return c
+
+    lax.fori_loop(0, 16, transpose_planes, 0, unroll=2)
+    send_planes(0, 8, 0)
+    lax.fori_loop(0, EARLY, step_four, 0, unroll=2)
+
+    bytes_of(recv_br.at[pl.ds(0, N - 1)], recv_sem.at[3]).wait()
+
+    def unpack_rest(r, c):
+        parts = [recv_br[pl.ds(r * 32 + q, 8, stride=4)].reshape(32, 128) for q in range(4)]
+        for b, part in enumerate(swap_bits(parts, 32, (2, 1))):
+            cells[pl.ds(4 * PITCH + 2 + 8 * r, 8), 4 * b:4 * b + 4, :] = part.reshape(8, 4, 128)
+        return c
+
+    lax.fori_loop(0, 4, unpack_rest, 0)
+    lax.fori_loop(16, 20, transpose_planes, 0, unroll=2)
+    send_planes(8, 2, 1)
+    take_near(0, 8)
+    take_near(8, 2)
+    lax.fori_loop(EARLY, 32, step_four, 0, unroll=2)
+    lax.fori_loop(0, 32, step_last, 0, unroll=4)
+
+    def add_face(face, part, fields):
+        b = pl.multiple_of(part * 8, 8)
+        spread, drift = factors(b)
+        code = face_code[face, pl.ds(b, 8), :]
+        coarse = code >= 4
+        first, second = code & 1, (code >> 1) & 1
+        if face >= 4:
+            first, second = second, first
+        low_first = coarse & (first == 0)
+        high_first = coarse & (first == 1)
+        fine_pick = ((lane >> 5) << 4) + second * 8 + ((lane & 15) >> 1)
+        picks = [jnp.where(coarse, 64 * half + fine_pick, lane) for half in range(2)]
+        sign = drift if face % 2 == 0 else -drift
+        ghost = {}
+        for f in fields:
+            rows = pl.ds(16 * face + b, 8)
+            half = [raw[2 * f + h, rows, :] + raw_far[2 * f + h, rows, :] for h in range(2)]
+            chosen = [jnp.where(high_first, half[1], half[0]), jnp.where(low_first, half[0], half[1])]
+            ghost[f] = [
+                jnp.take_along_axis(chosen[h], picks[h], axis=1, mode="promise_in_bounds") for h in range(2)]
+        for g in range(5):
+            for h in range(2):
                 flux = None
-                for a in range(3):
-                    for f in range(5):
-                        term = mix_s[g, a, f] * differences[f][a]
-                        flux = term if flux is None else flux + term
-                value = values[g][half] + (spread * sums[g] - drift * flux)
-                out[g, pl.ds(b, 8), pl.ds(pl.multiple_of((2 * i + half) * 128, 128), 128)] = value
-        return c
-
-    lax.fori_loop(0, 32, step, 0)
-
-    for at in range(4):
-        bytes_of(inbox.at[at], far_recv.at[at]).wait()
-    inbox_rows = inbox.reshape(50 * ROWS, 128)
-
-    def take_far(q, c):
-        base = table_s[4, q]
-        for h in range(10):
-            raw_far[h, pl.ds(q, 1), :] = inbox_rows[pl.ds(base + h * ROWS, 1), :]
-        return c
-
-    lax.fori_loop(0, 96, take_far, 0, unroll=4)
-
-    for face in range(6):
-        def add_face(part, c, face=face):
-            b = pl.multiple_of(part * 8, 8)
-            spread, drift = factors(b)
-            code = face_code[face, pl.ds(b, 8), :]
-            coarse = code >= 4
-            first, second = code & 1, (code >> 1) & 1
-            if face >= 4:
-                first, second = second, first
-            low_first = coarse & (first == 0)
-            high_first = coarse & (first == 1)
-            fine_pick = ((lane >> 5) << 4) + second * 8 + ((lane & 15) >> 1)
-            picks = [jnp.where(coarse, 64 * half + fine_pick, lane) for half in range(2)]
-            ghost = []
-            for f in range(5):
-                rows = pl.ds(16 * face + b, 8)
-                half = [raw[2 * f + h, rows, :] + raw_far[2 * f + h, rows, :] for h in range(2)]
-                chosen = [jnp.where(high_first, half[1], half[0]), jnp.where(low_first, half[0], half[1])]
-                ghost.append([
-                    jnp.take_along_axis(chosen[h], picks[h], axis=1, mode="promise_in_bounds")
-                    for h in range(2)])
-            for g in range(5):
-                for h in range(2):
-                    flux = None
-                    for f in range(5):
-                        term = mix_s[g, face // 2, f] * ghost[f][h]
-                        flux = term if flux is None else flux + term
-                    sign = drift if face % 2 == 0 else -drift
-                    value = spread * ghost[g][h] + sign * flux
-                    if face < 2:
-                        at = (30 * face + h) * 128
-                        out[g, pl.ds(b, 8), at:at + 128] = out[g, pl.ds(b, 8), at:at + 128] + value
-                    else:
-                        faces[face - 2, 2 * g + h, pl.ds(b, 8), :] = value
+                for f in fields:
+                    term = mix_s[g, face // 2, f] * ghost[f][h]
+                    flux = term if flux is None else flux + term
+                value = sign * flux
+                if g in fields:
+                    value = value + spread * ghost[g][h]
+                if face < 2:
+                    at = (30 * face + h) * 128
+                    out[g, pl.ds(b, 8), at:at + 128] = out[g, pl.ds(b, 8), at:at + 128] + value
+                elif 0 in fields:
+                    faces[face - 2, 2 * g + h, pl.ds(b, 8), :] = value
+                else:
+                    faces[face - 2, 2 * g + h, pl.ds(b, 8), :] = (
+                        faces[face - 2, 2 * g + h, pl.ds(b, 8), :] + value)
+
+    def add_planes(first, count, part, fields):
+        landed = (inbox, inbox_last)[part]
+        for at in range(4):
+            bytes_of(landed.at[at], far_recv.at[part, at]).wait()
+        landed_rows = landed.reshape(5 * count * ROWS, 128)
+
+        def take(q, c):
+            base = table_s[4 + 2 * part, q]
+            for h in range(count):
+                raw_far[first + h, pl.ds(q, 1), :] = landed_rows[pl.ds(base + h * ROWS, 1), :]
             return c
 
-        lax.fori_loop(0, 2, add_face, 0)
+        lax.fori_loop(0, 96, take, 0, unroll=4)
+        for face in range(6):
+            def add(part, c, face=face):
+                add_face(face, part, fields)
+                return c
+
+            lax.fori_loop(0, 2, add, 0, unroll=2)
+
+    add_planes(0, 8, 0, (0, 1, 2, 3))
+    add_planes(8, 2, 1, (4,))
 
     def spread_faces(at, c):
-        i, b = at >> 1, pl.multiple_of((at & 1) * 8, 8)
-        eighth = (i & 7) * 16
-        upper = i >> 3
-        for g in range(5):
+        g, b = at >> 1, pl.multiple_of((at & 1) * 8, 8)
+        halves = [[faces[f, 2 * g + h, pl.ds(b, 8), :] for h in range(2)] for f in range(4)]
+        after_second = [pltpu.roll(v, 112, 1) for v in halves[1]]
+        after_third = [pltpu.roll(v, 15, 1) for v in halves[3]]
+        for i in range(16):
+            both = jnp.where(lane >> 4 == i % 8, halves[0][i // 8], after_second[i // 8])
+            edge = pltpu.roll(both, (128 - 16 * (i % 8)) % 128, 1) if i % 8 else both
+            edges = (jnp.where(lane < 16, edge, 0.0), jnp.where(lane >= 112, edge, 0.0))
             for half in range(2):
-                cut = pl.ds(pl.multiple_of((2 * i + half) * 128, 128), 128)
-                lower_third = pltpu.roll(faces[2, 2 * g + half, pl.ds(b, 8), :], (128 - i) & 127, 1)
-                upper_third = pltpu.roll(faces[3, 2 * g + half, pl.ds(b, 8), :], 15 - i, 1)
-                value = out[g, pl.ds(b, 8), cut] + jnp.where(
-                    third == 0, lower_third, jnp.where(third == 15, upper_third, 0.0))
-                if half == 0:
-                    edge = pltpu.roll(faces[0, 2 * g + upper, pl.ds(b, 8), :], (128 - eighth) & 127, 1)
-                    value = value + jnp.where(lane < 16, edge, 0.0)
-                else:
-                    edge = pltpu.roll(faces[1, 2 * g + upper, pl.ds(b, 8), :], 112 - eighth, 1)
-                    value = value + jnp.where(lane >= 112, edge, 0.0)
-                out[g, pl.ds(b, 8), cut] = value
-        return c
-
-    lax.fori_loop(0, 32, spread_faces, 0)
+                cut = slice((2 * i + half) * 128, (2 * i + half + 1) * 128)
+                both = jnp.where(third == i, halves[2][half], after_third[half])
+                both = pltpu.roll(both, 128 - i, 1) if i else both
+                value = jnp.where((third == 0) | (third == 15), both, 0.0)
+                out[g, pl.ds(b, 8), cut] = out[g, pl.ds(b, 8), cut] + (value + edges[half])
+        return c
+
+    lax.fori_loop(0, 10, spread_faces, 0, unroll=2)
     bytes_of(recv_a.at[pl.ds(0, N - 1)], send_sem.at[0]).wait()
     for at, ref in ((1, send_ar), (2, send_b), (3, send_br)):
         bytes_of(ref.at[pl.ds(0, N - 1)], send_sem.at[at]).wait()
-    for at in range(4):
-        bytes_of(outbox.at[at], far_send.at[at]).wait()
+    for part, cut in enumerate((pl.ds(0, 8), pl.ds(8, 2))):
+        for at in range(4):
+            bytes_of(outbox.at[at, cut], far_send.at[part, at]).wait()
 
 
 def shards(old_state, old_map, new_map, box_level, ghost_list, coupling):
@@ -458,7 +497,8 @@
             pltpu.SMEM((8, 128), i32),
             pltpu.VMEM((49, 10, BOXES, 128), f32),
             pltpu.VMEM((4, 10, ROWS, 128), f32),
-            pltpu.VMEM((5, 10, ROWS, 128), f32),
+            pltpu.VMEM((5, 8, ROWS, 128), f32),
+            pltpu.VMEM((5, 2, ROWS, 128), f32),
             pltpu.VMEM((10, 96, 128), f32),
             pltpu.VMEM((10, 96, 128), f32),
             pltpu.VMEM((4, 10, BOXES, 128), f32),
@@ -466,8 +506,8 @@
             dma((4,)),
             dma((4,)),
             dma((2,)),
-            dma((4,)),
-            dma((4,)),
+            dma((2, 4)),
+            dma((2, 4)),
         ],
         compiler_params=pltpu.CompilerParams(
             collective_id=0, has_side_effects=True, vmem_limit_bytes=48 << 20),

time: 70 us -> 62.8 us (0.90)
  Pallas kernels: 63.6 us -> 56.3 us
    pallas_call x1, Pallas kernels: 63.6 us -> 56.3 us  [shards(): pl.pallas_call(kernel, out_shape=jax.ShapeDtypeStruct((5, BOXES, 4096), f...]
where the time goes in v4:
time: 62.8 us; the launch traced here: 62.4 us
  Pallas kernels  56.3 us (90%)
  local copies, waits for them, and re-layouts  6.09 us (10%)
    pallas_call x1, Pallas kernels, shards(): pl.pallas_call(kernel, out_shape=jax.ShapeDtypeStruct((5, BOXES, 4096), f...  56.3 us
    unnamed x13, local copies, waits for them, and re-layouts  6.09 us

profile of v4, /device:TPU:0, one launch (start us, length us, event | category | flops | bytes accessed | tf_op | source)
XLA Modules:
  0.0 62.4 jit_solution(9341071346470569236)
XLA Ops:
  0.0 0.0 copy-start
  0.0 1.3 %copy-done = f32[16,5,4096]{2,0,1:T(8,128)S(1)} copy-done((f32[16,5,4096]{2,0,1:T(8,128)S(1)}, f32[16,5,4096]{2,0,1:T(8,128)}, u32[]{:S(2)}) %copy-start) | copy-done | bytes 1310744
  1.3 0.0 copy-start.1
  1.3 0.9 %copy-done.1 = s32[2048,6,4]{0,2,1:T(4,128)S(1)} copy-done((s32[2048,6,4]{0,2,1:T(4,128)S(1)}, s32[2048,6,4]{0,2,1:T(4,128)}, u32[]{:S(2)}) %copy-start.1) | copy-done | bytes 196632
  2.2 0.0 copy-start.2
  2.2 0.7 %copy-done.2 = s32[2048]{0:T(1024)S(1)} copy-done((s32[2048]{0:T(1024)S(1)}, s32[2048]{0:T(1024)}, u32[]{:S(2)}) %copy-start.2) | copy-done | bytes 8216
  2.9 0.0 copy-start.3
  2.9 0.7 %copy-done.3 = f32[3,5,5]{2,0,1:T(4,128)S(1)} copy-done((f32[3,5,5]{2,0,1:T(4,128)S(1)}, f32[3,5,5]{2,0,1:T(4,128)}, u32[]{:S(2)}) %copy-start.3) | copy-done | bytes 324
  3.6 0.0 copy-start.4
  3.6 0.7 %copy-done.4 = s32[2048]{0:T(1024)S(1)} copy-done((s32[2048]{0:T(1024)S(1)}, s32[2048]{0:T(1024)}, u32[]{:S(2)}) %copy-start.4) | copy-done | bytes 8216
  4.3 0.0 copy-start.5
  4.3 0.7 %copy-done.5 = s32[2048]{0:T(1024)S(1)} copy-done((s32[2048]{0:T(1024)S(1)}, s32[2048]{0:T(1024)}, u32[]{:S(2)}) %copy-start.5) | copy-done | bytes 8216
  5.0 56.3 %shard_map.64 = f32[5,16,4096]{2,1,0:T(8,128)S(1)} custom-call(f32[5,16,4096]{2,1,0:T(8,128)S(1)} %bitcast.6, s32[2048]{0:T(1024)S(1)} %copy-done.4, s32[2048]{0:T(1024)S(1)} %copy-done.2, s32[16,128]{1,0:T(8,128)S(1)} %bitcast.8, s32[2048]{0:T(1024)S(1)} %copy-done.5, s32[6,4,2048]{2,1,0:T(4,128)S(1)} %bitcast.7, f32[5,3,5]{2,1,0:T(4,128)S(1)} %bitcast.9), custom_call_target="tpu_custom_call" | custom-call | tf_op jit(solution)/shard_map/pallas_call | solution.py:471
  61.4 1.1 %copy.8 = f32[16,5,4096]{2,0,1:T(8,128)} copy(f32[16,5,4096]{2,0,1:T(8,128)S(1)} %bitcast.5) | data formatting | bytes 2621440
Async XLA Ops:
  0.0 1.3 %copy-start = (f32[16,5,4096]{2,0,1:T(8,128)S(1)}, f32[16,5,4096]{2,0,1:T(8,128)}, u32[]{:S(2)}) copy-start(f32[16,5,4096]{2,0,1:T(8,128)} %param.6) | copy-start | bytes 3932164
  1.3 0.9 %copy-start.1 = (s32[2048,6,4]{0,2,1:T(4,128)S(1)}, s32[2048,6,4]{0,2,1:T(4,128)}, u32[]{:S(2)}) copy-start(s32[2048,6,4]{0,2,1:T(4,128)} %param.10) | copy-start | bytes 589828
  2.2 0.7 %copy-start.2 = (s32[2048]{0:T(1024)S(1)}, s32[2048]{0:T(1024)}, u32[]{:S(2)}) copy-start(s32[2048]{0:T(1024)} %new_map.1) | copy-start | bytes 24580
  2.9 0.7 %copy-start.3 = (f32[3,5,5]{2,0,1:T(4,128)S(1)}, f32[3,5,5]{2,0,1:T(4,128)}, u32[]{:S(2)}) copy-start(f32[3,5,5]{2,0,1:T(4,128)} %param.11) | copy-start | bytes 904
  3.6 0.7 %copy-start.4 = (s32[2048]{0:T(1024)S(1)}, s32[2048]{0:T(1024)}, u32[]{:S(2)}) copy-start(s32[2048]{0:T(1024)} %old_map.1) | copy-start | bytes 24580
  4.3 0.7 %copy-start.5 = (s32[2048]{0:T(1024)S(1)}, s32[2048]{0:T(1024)}, u32[]{:S(2)}) copy-start(s32[2048]{0:T(1024)} %box_level.1) | copy-start | bytes 24580

commit v5 on v4

--- a/solution.py
+++ b/solution.py
@@ -14,7 +14,7 @@
 ROWS = 24
 PITCH = 36
 BLOCK = 10 * BOXES
-EARLY = 24
+EARLY = 12
 diffusion_number = 0.12
 advection_number = 0.25
 
@@ -358,6 +358,7 @@
 
     lax.fori_loop(0, 16, transpose_planes, 0, unroll=2)
     send_planes(0, 8, 0)
+    take_near(0, 8)
     lax.fori_loop(0, EARLY, step_four, 0, unroll=2)
 
     bytes_of(recv_br.at[pl.ds(0, N - 1)], recv_sem.at[3]).wait()
@@ -371,7 +372,6 @@
     lax.fori_loop(0, 4, unpack_rest, 0)
     lax.fori_loop(16, 20, transpose_planes, 0, unroll=2)
     send_planes(8, 2, 1)
-    take_near(0, 8)
     take_near(8, 2)
     lax.fori_loop(EARLY, 32, step_four, 0, unroll=2)
     lax.fori_loop(0, 32, step_last, 0, unroll=4)

time: 62.8 us -> 62.2 us (level)
  no operation moved by 1% of the time
where the time goes in v5:
time: 62.2 us; the launch traced here: 61.9 us
  Pallas kernels  55.8 us (90%)
  local copies, waits for them, and re-layouts  6.09 us (10%)
    pallas_call x1, Pallas kernels, shards(): pl.pallas_call(kernel, out_shape=jax.ShapeDtypeStruct((5, BOXES, 4096), f...  55.8 us
    unnamed x13, local copies, waits for them, and re-layouts  6.09 us

profile of v5, /device:TPU:0, one launch (start us, length us, event | category | flops | bytes accessed | tf_op | source)
XLA Modules:
  0.0 61.9 jit_solution(9484129148169561432)
XLA Ops:
  0.0 0.0 copy-start
  0.0 1.3 %copy-done = f32[16,5,4096]{2,0,1:T(8,128)S(1)} copy-done((f32[16,5,4096]{2,0,1:T(8,128)S(1)}, f32[16,5,4096]{2,0,1:T(8,128)}, u32[]{:S(2)}) %copy-start) | copy-done | bytes 1310744
  1.3 0.0 copy-start.1
  1.3 0.9 %copy-done.1 = s32[2048,6,4]{0,2,1:T(4,128)S(1)} copy-done((s32[2048,6,4]{0,2,1:T(4,128)S(1)}, s32[2048,6,4]{0,2,1:T(4,128)}, u32[]{:S(2)}) %copy-start.1) | copy-done | bytes 196632
  2.2 0.0 copy-start.2
  2.2 0.7 %copy-done.2 = s32[2048]{0:T(1024)S(1)} copy-done((s32[2048]{0:T(1024)S(1)}, s32[2048]{0:T(1024)}, u32[]{:S(2)}) %copy-start.2) | copy-done | bytes 8216
  2.9 0.0 copy-start.3
  2.9 0.7 %copy-done.3 = f32[3,5,5]{2,0,1:T(4,128)S(1)} copy-done((f32[3,5,5]{2,0,1:T(4,128)S(1)}, f32[3,5,5]{2,0,1:T(4,128)}, u32[]{:S(2)}) %copy-start.3) | copy-done | bytes 324
  3.6 0.0 copy-start.4
  3.6 0.7 %copy-done.4 = s32[2048]{0:T(1024)S(1)} copy-done((s32[2048]{0:T(1024)S(1)}, s32[2048]{0:T(1024)}, u32[]{:S(2)}) %copy-start.4) | copy-done | bytes 8216
  4.3 0.0 copy-start.5
  4.3 0.7 %copy-done.5 = s32[2048]{0:T(1024)S(1)} copy-done((s32[2048]{0:T(1024)S(1)}, s32[2048]{0:T(1024)}, u32[]{:S(2)}) %copy-start.5) | copy-done | bytes 8216
  5.0 55.8 %shard_map.64 = f32[5,16,4096]{2,1,0:T(8,128)S(1)} custom-call(f32[5,16,4096]{2,1,0:T(8,128)S(1)} %bitcast.6, s32[2048]{0:T(1024)S(1)} %copy-done.4, s32[2048]{0:T(1024)S(1)} %copy-done.2, s32[16,128]{1,0:T(8,128)S(1)} %bitcast.8, s32[2048]{0:T(1024)S(1)} %copy-done.5, s32[6,4,2048]{2,1,0:T(4,128)S(1)} %bitcast.7, f32[5,3,5]{2,1,0:T(4,128)S(1)} %bitcast.9), custom_call_target="tpu_custom_call" | custom-call | tf_op jit(solution)/shard_map/pallas_call | solution.py:471
  60.9 1.1 %copy.8 = f32[16,5,4096]{2,0,1:T(8,128)} copy(f32[16,5,4096]{2,0,1:T(8,128)S(1)} %bitcast.5) | data formatting | bytes 2621440
Async XLA Ops:
  0.0 1.3 %copy-start = (f32[16,5,4096]{2,0,1:T(8,128)S(1)}, f32[16,5,4096]{2,0,1:T(8,128)}, u32[]{:S(2)}) copy-start(f32[16,5,4096]{2,0,1:T(8,128)} %param.6) | copy-start | bytes 3932164
  1.3 0.9 %copy-start.1 = (s32[2048,6,4]{0,2,1:T(4,128)S(1)}, s32[2048,6,4]{0,2,1:T(4,128)}, u32[]{:S(2)}) copy-start(s32[2048,6,4]{0,2,1:T(4,128)} %param.10) | copy-start | bytes 589828
  2.2 0.7 %copy-start.2 = (s32[2048]{0:T(1024)S(1)}, s32[2048]{0:T(1024)}, u32[]{:S(2)}) copy-start(s32[2048]{0:T(1024)} %new_map.1) | copy-start | bytes 24580
  2.9 0.7 %copy-start.3 = (f32[3,5,5]{2,0,1:T(4,128)S(1)}, f32[3,5,5]{2,0,1:T(4,128)}, u32[]{:S(2)}) copy-start(f32[3,5,5]{2,0,1:T(4,128)} %param.11) | copy-start | bytes 904
  3.6 0.7 %copy-start.4 = (s32[2048]{0:T(1024)S(1)}, s32[2048]{0:T(1024)}, u32[]{:S(2)}) copy-start(s32[2048]{0:T(1024)} %old_map.1) | copy-start | bytes 24580
  4.3 0.7 %copy-start.5 = (s32[2048]{0:T(1024)S(1)}, s32[2048]{0:T(1024)}, u32[]{:S(2)}) copy-start(s32[2048]{0:T(1024)} %box_level.1) | copy-start | bytes 24580

commit v6 on v5

--- a/solution.py
+++ b/solution.py
@@ -229,7 +229,7 @@
         put(send_b.at[d], cells.at[landing], send_sem.at[2], recv_sem.at[2], d)
         return c
 
-    lax.fori_loop(1, N, forward, 0)
+    lax.fori_loop(1, N, forward, 0, unroll=4)
     gather(me, cells.at[landing])
     bytes_of(recv_ar.at[pl.ds(0, N - 1)], recv_sem.at[1]).wait()
 
@@ -257,7 +257,7 @@
         put(send_br.at[d], recv_br.at[me], send_sem.at[3], recv_sem.at[3], d)
         return c
 
-    lax.fori_loop(1, N, forward_rest, 0)
+    lax.fori_loop(1, N, forward_rest, 0, unroll=4)
     gather_rest(me, recv_br.at[me])
     bytes_of(cells.at[pl.ds(0, N - 1)], recv_sem.at[2]).wait()
 

time: 62.2 us -> 62.5 us (level)
  no operation moved by 1% of the time
where the time goes in v6:
time: 62.5 us; the launch traced here: 62.2 us
  Pallas kernels  56.1 us (90%)
  local copies, waits for them, and re-layouts  6.09 us (10%)
    pallas_call x1, Pallas kernels, shards(): pl.pallas_call(kernel, out_shape=jax.ShapeDtypeStruct((5, BOXES, 4096), f...  56.1 us
    unnamed x13, local copies, waits for them, and re-layouts  6.09 us

profile of v6, /device:TPU:0, one launch (start us, length us, event | category | flops | bytes accessed | tf_op | source)
XLA Modules:
  0.0 62.2 jit_solution(9500702285295954986)
XLA Ops:
  0.0 0.0 copy-start
  0.0 1.3 %copy-done = f32[16,5,4096]{2,0,1:T(8,128)S(1)} copy-done((f32[16,5,4096]{2,0,1:T(8,128)S(1)}, f32[16,5,4096]{2,0,1:T(8,128)}, u32[]{:S(2)}) %copy-start) | copy-done | bytes 1310744
  1.3 0.0 copy-start.1
  1.3 0.9 %copy-done.1 = s32[2048,6,4]{0,2,1:T(4,128)S(1)} copy-done((s32[2048,6,4]{0,2,1:T(4,128)S(1)}, s32[2048,6,4]{0,2,1:T(4,128)}, u32[]{:S(2)}) %copy-start.1) | copy-done | bytes 196632
  2.2 0.0 copy-start.2
  2.2 0.7 %copy-done.2 = s32[2048]{0:T(1024)S(1)} copy-done((s32[2048]{0:T(1024)S(1)}, s32[2048]{0:T(1024)}, u32[]{:S(2)}) %copy-start.2) | copy-done | bytes 8216
  2.9 0.0 copy-start.3
  2.9 0.7 %copy-done.3 = f32[3,5,5]{2,0,1:T(4,128)S(1)} copy-done((f32[3,5,5]{2,0,1:T(4,128)S(1)}, f32[3,5,5]{2,0,1:T(4,128)}, u32[]{:S(2)}) %copy-start.3) | copy-done | bytes 324
  3.6 0.0 copy-start.4
  3.6 0.7 %copy-done.4 = s32[2048]{0:T(1024)S(1)} copy-done((s32[2048]{0:T(1024)S(1)}, s32[2048]{0:T(1024)}, u32[]{:S(2)}) %copy-start.4) | copy-done | bytes 8216
  4.3 0.0 copy-start.5
  4.3 0.7 %copy-done.5 = s32[2048]{0:T(1024)S(1)} copy-done((s32[2048]{0:T(1024)S(1)}, s32[2048]{0:T(1024)}, u32[]{:S(2)}) %copy-start.5) | copy-done | bytes 8216
  5.0 56.1 %shard_map.64 = f32[5,16,4096]{2,1,0:T(8,128)S(1)} custom-call(f32[5,16,4096]{2,1,0:T(8,128)S(1)} %bitcast.6, s32[2048]{0:T(1024)S(1)} %copy-done.4, s32[2048]{0:T(1024)S(1)} %copy-done.2, s32[16,128]{1,0:T(8,128)S(1)} %bitcast.8, s32[2048]{0:T(1024)S(1)} %copy-done.5, s32[6,4,2048]{2,1,0:T(4,128)S(1)} %bitcast.7, f32[5,3,5]{2,1,0:T(4,128)S(1)} %bitcast.9), custom_call_target="tpu_custom_call" | custom-call | tf_op jit(solution)/shard_map/pallas_call | solution.py:471
  61.1 1.1 %copy.8 = f32[16,5,4096]{2,0,1:T(8,128)} copy(f32[16,5,4096]{2,0,1:T(8,128)S(1)} %bitcast.5) | data formatting | bytes 2621440
Async XLA Ops:
  0.0 1.3 %copy-start = (f32[16,5,4096]{2,0,1:T(8,128)S(1)}, f32[16,5,4096]{2,0,1:T(8,128)}, u32[]{:S(2)}) copy-start(f32[16,5,4096]{2,0,1:T(8,128)} %param.6) | copy-start | bytes 3932164
  1.3 0.9 %copy-start.1 = (s32[2048,6,4]{0,2,1:T(4,128)S(1)}, s32[2048,6,4]{0,2,1:T(4,128)}, u32[]{:S(2)}) copy-start(s32[2048,6,4]{0,2,1:T(4,128)} %param.10) | copy-start | bytes 589828
  2.2 0.7 %copy-start.2 = (s32[2048]{0:T(1024)S(1)}, s32[2048]{0:T(1024)}, u32[]{:S(2)}) copy-start(s32[2048]{0:T(1024)} %new_map.1) | copy-start | bytes 24580
  2.9 0.7 %copy-start.3 = (f32[3,5,5]{2,0,1:T(4,128)S(1)}, f32[3,5,5]{2,0,1:T(4,128)}, u32[]{:S(2)}) copy-start(f32[3,5,5]{2,0,1:T(4,128)} %param.11) | copy-start | bytes 904
  3.6 0.7 %copy-start.4 = (s32[2048]{0:T(1024)S(1)}, s32[2048]{0:T(1024)}, u32[]{:S(2)}) copy-start(s32[2048]{0:T(1024)} %old_map.1) | copy-start | bytes 24580
  4.3 0.7 %copy-start.5 = (s32[2048]{0:T(1024)S(1)}, s32[2048]{0:T(1024)}, u32[]{:S(2)}) copy-start(s32[2048]{0:T(1024)} %box_level.1) | copy-start | bytes 24580
